TPU v7x, 32 devices: a whole 2x2x4 slice. The times are simulated.
32 devices in a mesh: fsdp: 16 (over z, y, x), ctx: 2 (over core).
Axes of the slice: x: 2, y: 2, z: 4, core: 2. Of those that a mesh axis runs over, the one named last changes fastest.
Arguments:
- tokens: bfloat16 [16, 2, 512, 768], P('fsdp', 'ctx'), may hold values from -6 to 6
- pair_order: int32 [16, 2], P('fsdp'), may hold values from 0 to 1, each once within a row
- gain_one: bfloat16 [768], P('fsdp'), may hold values from 0.5 to 1.5
- bias_one: bfloat16 [768], P('fsdp'), may hold values from -3 to 3
- w_qkv: bfloat16 [768, 2304], P('fsdp'), may hold values from -0.21875 to 0.21875
- bias_q: bfloat16 [768], P('fsdp'), may hold values from -3 to 3
- bias_v: bfloat16 [768], P('fsdp'), may hold values from -3 to 3
- w_out: bfloat16 [768, 768], P('fsdp'), may hold values from -0.875 to 0.875
- bias_out: bfloat16 [768], P('fsdp'), may hold values from -3 to 3
- gain_two: bfloat16 [768], P('fsdp'), may hold values from 0.5 to 1.5
- bias_two: bfloat16 [768], P('fsdp'), may hold values from -3 to 3
- w_fc: bfloat16 [768, 3072], P('fsdp'), may hold values from -0.21875 to 0.21875
- bias_fc: bfloat16 [3072], P('fsdp'), may hold values from -3 to 3
- w_proj: bfloat16 [3072, 768], P('fsdp'), may hold values from -0.109375 to 0.109375
- bias_proj: bfloat16 [768], P('fsdp'), may hold values from -3 to 3
- cotangent: bfloat16 [16, 2, 512, 768], P('fsdp', 'ctx'), may hold values from -6 to 6
Outputs:
- layer_out: bfloat16 [16, 2, 512, 768], P('fsdp', 'ctx')
- grad_tokens: float32 [16, 2, 512, 768], P('fsdp', 'ctx')
- grad_gain_one: float32 [768], P(('fsdp', 'ctx'))
- grad_bias_one: float32 [768], P(('fsdp', 'ctx'))
- grad_w_qkv: float32 [768, 2304], P(('fsdp', 'ctx'))
- grad_bias_q: float32 [768], P(('fsdp', 'ctx'))
- grad_bias_v: float32 [768], P(('fsdp', 'ctx'))
- grad_w_out: float32 [768, 768], P(('fsdp', 'ctx'))
- grad_bias_out: float32 [768], P(('fsdp', 'ctx'))
- grad_gain_two: float32 [768], P(('fsdp', 'ctx'))
- grad_bias_two: float32 [768], P(('fsdp', 'ctx'))
- grad_w_fc: float32 [768, 3072], P(('fsdp', 'ctx'))
- grad_bias_fc: float32 [3072], P(('fsdp', 'ctx'))
- grad_w_proj: float32 [3072, 768], P(('fsdp', 'ctx'))
- grad_bias_proj: float32 [768], P(('fsdp', 'ctx'))
Inputs may be any that keep to these rules, and one draw needn't show every extreme that they name: `pair_order`: each row is a permutation of 0 to 1.
All inputs are finite; a program needn't handle non-finite values.
Results may differ from a plain program's by a relative error of at most 0.013.
Values may be sent and summed in bfloat16 or wider, within the bound.
No kernel may reach another device: no remote copies, remote signals or barrier semaphores. Data moves between devices by JAX's collectives and lax.ppermute only.
A program may use at most 192 MiB of HBM per device.

v0:
```python
import jax
import jax.numpy as jnp
from jax import lax
from jax.sharding import PartitionSpec as P

HEADS = 12
HEAD_DIM = 64


EPSILON = 1e-05
NEG_FILL = -1e30


def layer_norm(values, norm_gain, norm_bias):
    average = jnp.mean(values, axis=-1, keepdims=True)
    centred = values - average
    variance = jnp.mean(centred * centred, axis=-1, keepdims=True)
    return centred * lax.rsqrt(variance + EPSILON) * norm_gain + norm_bias


def gelu_tanh(values):
    return jax.nn.gelu(values, approximate=True)


def block_places(pair_order, block_len):
    count = pair_order.shape[1]
    starts = jnp.stack([pair_order, 2 * count - 1 - pair_order], axis=2) * block_len
    offsets = jnp.arange(block_len, dtype=jnp.int32)
    placed = starts[:, :, :, None] + offsets
    return placed.reshape(pair_order.shape[0], count * 2 * block_len)


def to_heads(array):
    split = array.reshape(array.shape[0], array.shape[1], HEADS, HEAD_DIM)
    return jnp.moveaxis(split, 2, 0)


def from_heads(array):
    moved = jnp.moveaxis(array, 0, 2)
    return moved.reshape(moved.shape[0], moved.shape[1], HEADS * HEAD_DIM)


def inner_rows(left, right):
    return lax.dot_general(
        left, right, (((0,), (0,)), ((), ())), preferred_element_type=jnp.float32
    )


def times_t(left, right):
    return lax.dot_general(
        left, right, (((1,), (1,)), ((), ())), preferred_element_type=jnp.float32
    )


def body(
    tokens,
    pair_order,
    gain_one,
    bias_one,
    w_qkv,
    bias_q,
    bias_v,
    w_out,
    bias_out,
    gain_two,
    bias_two,
    w_fc,
    bias_fc,
    w_proj,
    bias_proj,
    cotangent,
):
    seq_count, unused, length, model_width = tokens.shape
    block_len = length // 2
    ctx_index = lax.axis_index("ctx")
    score_scale = HEAD_DIM ** (-0.5)
    gathered = (
        lax.all_gather(gain_one, "fsdp", axis=0, tiled=True),
        lax.all_gather(bias_one, "fsdp", axis=0, tiled=True),
        lax.all_gather(w_qkv, "fsdp", axis=0, tiled=True),
        lax.all_gather(bias_q, "fsdp", axis=0, tiled=True),
        lax.all_gather(bias_v, "fsdp", axis=0, tiled=True),
        lax.all_gather(w_out, "fsdp", axis=0, tiled=True),
        lax.all_gather(bias_out, "fsdp", axis=0, tiled=True),
        lax.all_gather(gain_two, "fsdp", axis=0, tiled=True),
        lax.all_gather(bias_two, "fsdp", axis=0, tiled=True),
        lax.all_gather(w_fc, "fsdp", axis=0, tiled=True),
        lax.all_gather(bias_fc, "fsdp", axis=0, tiled=True),
        lax.all_gather(w_proj, "fsdp", axis=0, tiled=True),
        lax.all_gather(bias_proj, "fsdp", axis=0, tiled=True),
    )
    (
        gain_first,
        bias_first,
        qkv_full,
        query_bias,
        value_bias,
        out_full,
        out_bias,
        gain_second,
        bias_second,
        fc_full,
        fc_bias,
        proj_full,
        proj_bias,
    ) = [member.astype(jnp.float32) if member.ndim == 1 else member for member in gathered]
    flat_rows = tokens.astype(jnp.float32).reshape(seq_count * length, model_width)
    norm_first, pull_first = jax.vjp(layer_norm, flat_rows, gain_first, bias_first)
    normed = norm_first.astype(jnp.bfloat16)
    project = jnp.dot(normed, qkv_full, preferred_element_type=jnp.float32)
    queries = (
        (project[:, :model_width] + query_bias)
        .astype(jnp.bfloat16)
        .reshape(seq_count, length, model_width)
    )
    keys_own = (
        project[:, model_width : 2 * model_width]
        .astype(jnp.bfloat16)
        .reshape(seq_count, length, model_width)
    )
    values_own = (
        (project[:, 2 * model_width :] + value_bias)
        .astype(jnp.bfloat16)
        .reshape(seq_count, length, model_width)
    )
    keys_all, values_all = (
        lax.all_gather(keys_own, "ctx", axis=1, tiled=True),
        lax.all_gather(values_own, "ctx", axis=1, tiled=True),
    )
    all_places = block_places(pair_order, block_len)
    own_places = lax.dynamic_slice_in_dim(all_places, ctx_index * length, length, 1)
    allowed = own_places[:, :, None] >= all_places[:, None, :]
    query_heads = to_heads(queries)
    key_heads = to_heads(keys_all)
    value_heads = to_heads(values_all)

    def head_forward(member):
        query_h, key_h, value_h = member
        scores = (
            jnp.einsum("sqd,skd->sqk", query_h, key_h, preferred_element_type=jnp.float32)
            * score_scale
        )
        scores = jnp.where(allowed, scores, NEG_FILL)
        row_top = jnp.max(scores, axis=-1, keepdims=True)
        exponent = jnp.exp(scores - row_top)
        row_sum = jnp.sum(exponent, axis=-1, keepdims=True)
        chances = (exponent / row_sum).astype(jnp.bfloat16)
        output = jnp.einsum("sqk,skd->sqd", chances, value_h, preferred_element_type=jnp.float32)
        return (output, (row_top + jnp.log(row_sum))[..., 0])

    head_out, log_total = lax.map(head_forward, (query_heads, key_heads, value_heads))
    mixed = from_heads(head_out).astype(jnp.bfloat16).reshape(seq_count * length, model_width)
    branch = jnp.dot(mixed, out_full, preferred_element_type=jnp.float32) + out_bias
    middle = flat_rows + branch
    norm_second, pull_second = jax.vjp(layer_norm, middle, gain_second, bias_second)
    normed_two = norm_second.astype(jnp.bfloat16)
    hidden_pre = jnp.dot(normed_two, fc_full, preferred_element_type=jnp.float32) + fc_bias
    active_full, pull_gelu = jax.vjp(gelu_tanh, hidden_pre)
    active = active_full.astype(jnp.bfloat16)
    result_rows = (
        middle + jnp.dot(active, proj_full, preferred_element_type=jnp.float32) + proj_bias
    )
    out_tokens = result_rows.astype(jnp.bfloat16).reshape(tokens.shape)
    grad_rows = cotangent.reshape(seq_count * length, model_width)
    grad_float = grad_rows.astype(jnp.float32)
    grad_proj = inner_rows(active, grad_rows)
    sum_proj_bias = jnp.sum(grad_float, axis=0)
    d_active = times_t(grad_rows, proj_full)
    d_pre = pull_gelu(d_active)[0].astype(jnp.bfloat16)
    grad_fc = inner_rows(normed_two, d_pre)
    sum_fc_bias = jnp.sum(d_pre.astype(jnp.float32), axis=0)
    d_normed_two = times_t(d_pre, fc_full)
    d_middle_norm, grad_gain_second, grad_bias_second = pull_second(d_normed_two)
    d_middle = grad_float + d_middle_norm
    d_branch = d_middle.astype(jnp.bfloat16)
    grad_out_w = inner_rows(mixed, d_branch)
    sum_out_bias = jnp.sum(d_branch.astype(jnp.float32), axis=0)
    d_mixed = (
        times_t(d_branch, out_full).astype(jnp.bfloat16).reshape(seq_count, length, model_width)
    )
    dmix_heads = to_heads(d_mixed)

    def score_grads(query_h, key_h, value_h, dmix_h, lse_h, mask):
        scores = (
            jnp.einsum("sqd,skd->sqk", query_h, key_h, preferred_element_type=jnp.float32)
            * score_scale
        )
        prob_full = jnp.exp(jnp.where(mask, scores, NEG_FILL) - lse_h[..., None])
        d_probs = jnp.einsum("sqd,skd->sqk", dmix_h, value_h, preferred_element_type=jnp.float32)
        delta = jnp.sum(prob_full * d_probs, axis=-1)
        return (prob_full, d_probs, delta)

    def head_back_keys(member):
        query_h, key_h, value_h, dmix_h, lse_h = member
        prob_full, d_probs, delta = score_grads(query_h, key_h, value_h, dmix_h, lse_h, allowed)
        d_scores = (prob_full * (d_probs - delta[..., None])).astype(jnp.bfloat16)
        d_query = (
            jnp.einsum("sqk,skd->sqd", d_scores, key_h, preferred_element_type=jnp.float32)
            * score_scale
        )
        d_key = (
            jnp.einsum("sqk,sqd->skd", d_scores, query_h, preferred_element_type=jnp.float32)
            * score_scale
        )
        d_value = jnp.einsum(
            "sqk,sqd->skd",
            prob_full.astype(jnp.bfloat16),
            dmix_h,
            preferred_element_type=jnp.float32,
        )
        return (d_query, d_key, d_value)

    dq_heads, dk_heads, dv_heads = lax.map(
        head_back_keys, (query_heads, key_heads, value_heads, dmix_heads, log_total)
    )
    d_key_own, d_value_own = (
        lax.psum_scatter(
            from_heads(dk_heads).astype(jnp.bfloat16), "ctx", scatter_dimension=1, tiled=True
        ).astype(jnp.float32),
        lax.psum_scatter(
            from_heads(dv_heads).astype(jnp.bfloat16), "ctx", scatter_dimension=1, tiled=True
        ).astype(jnp.float32),
    )
    d_query_all = from_heads(dq_heads).astype(jnp.bfloat16)
    d_key_round = d_key_own.astype(jnp.bfloat16)
    d_value_round = d_value_own.astype(jnp.bfloat16)
    d_qkv = jnp.concatenate([d_query_all, d_key_round, d_value_round], axis=-1).reshape(
        seq_count * length, 3 * model_width
    )
    grad_qkv = inner_rows(normed, d_qkv)
    sum_query_bias = jnp.sum(d_query_all.astype(jnp.float32), axis=(0, 1))
    sum_value_bias = jnp.sum(d_value_round.astype(jnp.float32), axis=(0, 1))
    d_normed = times_t(d_qkv, qkv_full)
    d_rows_norm, grad_gain_first, grad_bias_first = pull_first(d_normed)
    grad_inputs = (d_middle + d_rows_norm).reshape(tokens.shape)
    shares = (
        lax.psum_scatter(grad_gain_first, ("fsdp", "ctx"), scatter_dimension=0, tiled=True),
        lax.psum_scatter(grad_bias_first, ("fsdp", "ctx"), scatter_dimension=0, tiled=True),
        lax.psum_scatter(grad_qkv, ("fsdp", "ctx"), scatter_dimension=0, tiled=True),
        lax.psum_scatter(sum_query_bias, ("fsdp", "ctx"), scatter_dimension=0, tiled=True),
        lax.psum_scatter(sum_value_bias, ("fsdp", "ctx"), scatter_dimension=0, tiled=True),
        lax.psum_scatter(grad_out_w, ("fsdp", "ctx"), scatter_dimension=0, tiled=True),
        lax.psum_scatter(sum_out_bias, ("fsdp", "ctx"), scatter_dimension=0, tiled=True),
        lax.psum_scatter(grad_gain_second, ("fsdp", "ctx"), scatter_dimension=0, tiled=True),
        lax.psum_scatter(grad_bias_second, ("fsdp", "ctx"), scatter_dimension=0, tiled=True),
        lax.psum_scatter(grad_fc, ("fsdp", "ctx"), scatter_dimension=0, tiled=True),
        lax.psum_scatter(sum_fc_bias, ("fsdp", "ctx"), scatter_dimension=0, tiled=True),
        lax.psum_scatter(grad_proj, ("fsdp", "ctx"), scatter_dimension=0, tiled=True),
        lax.psum_scatter(sum_proj_bias, ("fsdp", "ctx"), scatter_dimension=0, tiled=True),
    )
    (
        share_gain_one,
        share_bias_one,
        share_qkv,
        share_bias_q,
        share_bias_v,
        share_out,
        share_bias_out,
        share_gain_two,
        share_bias_two,
        share_fc,
        share_bias_fc,
        share_proj,
        share_bias_proj,
    ) = shares
    return (
        out_tokens,
        grad_inputs,
        share_gain_one,
        share_bias_one,
        share_qkv,
        share_bias_q,
        share_bias_v,
        share_out,
        share_bias_out,
        share_gain_two,
        share_bias_two,
        share_fc,
        share_bias_fc,
        share_proj,
        share_bias_proj,
    )


def solution(mesh):
    placed = (
        P("fsdp", "ctx", None, None),
        P("fsdp", None),
        P("fsdp"),
        P("fsdp"),
        P("fsdp", None),
        P("fsdp"),
        P("fsdp"),
        P("fsdp", None),
        P("fsdp"),
        P("fsdp"),
        P("fsdp"),
        P("fsdp", None),
        P("fsdp"),
        P("fsdp", None),
        P("fsdp"),
        P("fsdp", "ctx", None, None),
    )
    return jax.shard_map(
        body,
        mesh=mesh,
        in_specs=placed,
        out_specs=(
            P("fsdp", "ctx", None, None),
            P("fsdp", "ctx", None, None),
            P(("fsdp", "ctx")),
            P(("fsdp", "ctx")),
            P(("fsdp", "ctx"), None),
            P(("fsdp", "ctx")),
            P(("fsdp", "ctx")),
            P(("fsdp", "ctx"), None),
            P(("fsdp", "ctx")),
            P(("fsdp", "ctx")),
            P(("fsdp", "ctx")),
            P(("fsdp", "ctx"), None),
            P(("fsdp", "ctx")),
            P(("fsdp", "ctx"), None),
            P(("fsdp", "ctx")),
        ),
        check_vma=False,
    )
```

profile of v0, /device:TPU:1, one launch (start us, length us, event | category | flops | bytes accessed | tf_op | source)
XLA Modules:
  0.0 1013.3 jit_solution(11505592974098191568)
XLA Ops:
  18.1 64.8 %all-reduce.19 = (bf16[768]{0:T(1024)(128)(2,1)S(1)}, bf16[768]{0:T(1024)(128)(2,1)S(1)}, bf16[768]{0:T(1024)(128)(2,1)S(1)}, bf16[768]{0:T(1024)(128)(2,1)S(1)}...) all-reduce(bf16[768]{0:T(1024)(128)(2,1)S(1)} %dynamic-update-slice, ...), channel_id=1, replica_groups=mesh['fsdp'=16,'ctx'=2] {'fsdp'}, use_global_device_ids=true, to_apply=%add.1 | all-reduce | flops 9216 | bytes 36864
  85.7 4.4 fusion.72
  90.1 2.1 copy-done.3
  93.3 3.0 fusion.64
  99.7 13.9 %all-gather.17.cloned.1.call-done = bf16[1024,768]{1,0:T(8,128)(2,1)} async-done(((bf16[512,768]{1,0:T(8,128)(2,1)}), bf16[1024,768]{1,0:T(8,128)(2,1)}) %all-gather.17.cloned.1.call-update) | async-done | bytes 1572880 | tf_op jit(solution)/shard_map/all_gather | solution.py:127
  115.3 2.8 copy.53
  118.1 8.7 all-gather.19.cloned.1.call-done
  128.5 2.8 copy.54
  131.4 43.8 %while.28 = (s32[]{:T(128)}, bf16[12,1,512,64]{2,3,1,0:T(8,128)(2,1)S(1)}, f32[12,1,512]{2,1,0:T(1,128)S(1)}, bf16[12,1,512,64]{3,2,1,0:T(8,128)(2,1)S(1)}, bf16...) while((s32[]{:T(128)}, ...), condition=%wide.region_5.6_spmd.clone, body=%wide.region_2.5_spmd.clone.sunk | while | flops 138935808 | bytes 7106665 | solution.py:151
  175.2 9.5 all-gather.11.cloned.1.call-done
  184.7 2.4 fusion.100
  187.5 80.2 %all-gather.13.cloned.1.call-done = bf16[768,3072]{1,0:T(8,128)(2,1)} async-done(((bf16[48,3072]{1,0:T(8,128)(2,1)}), bf16[768,3072]{1,0:T(8,128)(2,1)}) %all-gather.13.cloned.1.call-update) | async-done | bytes 4718608 | tf_op jit(solution)/shard_map/all_gather | solution.py:87
  267.7 7.0 fusion.95
  274.7 74.8 %all-gather.15.cloned.1.call-done = bf16[3072,768]{1,0:T(8,128)(2,1)} async-done(((bf16[192,768]{1,0:T(8,128)(2,1)}), bf16[3072,768]{1,0:T(8,128)(2,1)}) %all-gather.15.cloned.1.call-update) | async-done | bytes 4718608 | tf_op jit(solution)/shard_map/all_gather | solution.py:89
  349.5 9.4 convert_reduce_fusion
  358.9 3.0 multiply_reduce_fusion.1
  361.9 2.0 fusion.98
  367.2 104.6 %while.29 = (s32[]{:T(128)}, bf16[12,1,512,64]{2,3,1,0:T(8,128)(2,1)S(1)}, bf16[12,1,1024,64]{2,3,1,0:T(8,128)(2,1)}, bf16[12,1,1024,64]{2,3,1,0:T(8,128)(2,1)},...) while((s32[]{:T(128)}, ...), condition=%wide.region_12.13_spmd.clone, body=%wide.region_10.12_spmd.clone.sunk | while | flops 340884992 | bytes 17585280 | solution.py:213
  368.7 1.9 multiply_reduce_fusion.5
  372.3 1.9 fusion.148
  374.2 1.8 fusion.149
  377.5 1.9 multiply_reduce_fusion.5
  381.0 1.9 fusion.148
  386.2 1.9 multiply_reduce_fusion.5
  389.7 1.9 fusion.148
  391.6 1.8 fusion.149
  394.9 1.9 multiply_reduce_fusion.5
  398.4 1.9 fusion.148
  400.3 1.8 fusion.149
  403.6 1.9 multiply_reduce_fusion.5
  407.2 1.9 fusion.148
  412.3 1.9 multiply_reduce_fusion.5
  415.9 1.9 fusion.148
  417.8 1.8 fusion.149
  421.0 1.9 multiply_reduce_fusion.5
  424.6 1.9 fusion.148
  426.5 1.8 fusion.149
  429.8 1.9 multiply_reduce_fusion.5
  433.3 1.9 fusion.148
  435.2 1.8 fusion.149
  438.5 1.9 multiply_reduce_fusion.5
  442.0 1.9 fusion.148
  447.2 1.9 multiply_reduce_fusion.5
  450.7 1.9 fusion.148
  452.6 1.8 fusion.149
  455.9 1.9 multiply_reduce_fusion.5
  459.5 1.9 fusion.148
  464.6 1.9 multiply_reduce_fusion.5
  468.2 1.9 fusion.148
  470.1 1.8 fusion.149
  472.7 3.6 fusion.101
  476.4 4.6 reduce-scatter.9.cloned.1.call-done
  481.0 12.6 %reduce-scatter.7.cloned.1.call-done = bf16[1,512,768]{1,2,0:T(8,128)(2,1)} async-done(((bf16[1,1024,768]{1,2,0:T(8,128)(2,1)}), bf16[1,512,768]{1,2,0:T(8,128)(2,1)}) %reduce-scatter.7.cloned.1.call-update) | async-done | bytes 786448 | tf_op jit(solution)/shard_map/reduce_scatter | solution.py:217
  493.6 6.6 fusion.68
  500.3 8.9 fusion.94
  509.5 10.4 %fusion.74 = f32[3072,768]{1,0:T(8,128)} fusion(bf16[1,1,512,768]{3,2,1,0:T(8,128)(2,1)} %param.35, f32[512,3072]{1,0:T(8,128)} %fusion.95, f32[3072]{0:T(1024)S(1)} %convert_element_type.179), kind=kOutput, calls=%fused_computation.108 | convolution fusion | flops 2431647744 | bytes 16527360 | tf_op jit(solution)/shard_map/dot_general | solution.py:44
  520.2 9.8 fusion.66
  530.2 2.3 fusion.96
  533.6 1.9 convert_reduce_fusion.2
  535.6 41.1 %all-reduce.18 = (f32[768]{0:T(1024)S(1)}, f32[768]{0:T(1024)S(1)}, f32[768]{0:T(1024)S(1)}, f32[768]{0:T(1024)S(1)}, f32[768]{0:T(1024)S(1)}, /*index=5*/f32[76...) all-reduce(f32[768]{0:T(1024)S(1)} %get-tuple-element.198, ...), channel_id=6, replica_groups=mesh['fsdp'=16,'ctx'=2] {'fsdp','ctx'}, use_global_device_ids=true, to_apply=%region_18.19.clone | all-reduce | flops 9216 | bytes 73728
  582.0 16.0 %reduce-scatter.13.cloned.1.call-done = f32[24,768]{1,0:T(8,128)} async-done(((f32[768,768]{1,0:T(8,128)}), f32[24,768]{1,0:T(8,128)}) %reduce-scatter.13.cloned.1.call-update) | async-done | bytes 73744 | tf_op jit(solution)/shard_map/reduce_scatter | solution.py:242
  597.9 125.1 %reduce-scatter.11.cloned.1.call-done = f32[24,2304]{1,0:T(8,128)} async-done(((f32[768,2304]{1,0:T(8,128)}), f32[24,2304]{1,0:T(8,128)}) %reduce-scatter.11.cloned.1.call-update) | async-done | bytes 221200 | tf_op jit(solution)/shard_map/reduce_scatter | solution.py:239
  723.0 141.0 %reduce-scatter.15.cloned.1.call-done = f32[24,3072]{1,0:T(8,128)} async-done(((f32[768,3072]{1,0:T(8,128)}), f32[24,3072]{1,0:T(8,128)}) %reduce-scatter.15.cloned.1.call-update) | async-done | bytes 294928 | tf_op jit(solution)/shard_map/reduce_scatter | solution.py:246
  864.0 142.0 %reduce-scatter.17.cloned.1.call-done = f32[96,768]{1,0:T(8,128)} async-done(((f32[3072,768]{1,0:T(8,128)}), f32[96,768]{1,0:T(8,128)}) %reduce-scatter.17.cloned.1.call-update) | async-done | bytes 294928 | tf_op jit(solution)/shard_map/reduce_scatter | solution.py:248
  (238 shorter events, 120.0 us)
Async XLA Ops:
  7.2 78.5 %all-gather.9.cloned.1.call-start = ((), (), s32[]{:S(2)}) async-start(), calls=%async_computation.6 | async-start | bytes 3760128 | tf_op jit(solution)/shard_map/all_gather | solution.py:80
  7.9 105.7 %all-gather.17.cloned.1.call-start = ((), (), s32[]{:S(2)}) async-start(), calls=%async_computation.16 | async-start | bytes 2359296 | tf_op jit(solution)/shard_map/all_gather | solution.py:127
  90.1 2.1 copy-start.3
  93.2 33.6 %all-gather.19.cloned.1.call-start = ((), (), s32[]{:S(2)}) async-start(), calls=%async_computation.17 | async-start | bytes 2359296 | tf_op jit(solution)/shard_map/all_gather | solution.py:128
  93.3 5.1 copy-start.9
  96.3 88.4 %all-gather.11.cloned.1.call-start = ((), (), s32[]{:S(2)}) async-start(), calls=%async_computation.7 | async-start | bytes 1253376 | tf_op jit(solution)/shard_map/all_gather | solution.py:83
  96.9 170.8 %all-gather.13.cloned.1.call-start = ((), (), s32[]{:S(2)}) async-start(), calls=%async_computation.8 | async-start | bytes 5013504 | tf_op jit(solution)/shard_map/all_gather | solution.py:87
  97.5 252.0 %all-gather.15.cloned.1.call-start = ((), (), s32[]{:S(2)}) async-start(), calls=%async_computation.9 | async-start | bytes 5013504 | tf_op jit(solution)/shard_map/all_gather | solution.py:89
  98.1 382.9 %reduce-scatter.9.cloned.1.call-start = ((), (), s32[]{:S(2)}) async-start(), calls=%async_computation.11 | async-start | bytes 2359296 | tf_op jit(solution)/shard_map/reduce_scatter | solution.py:220
  131.3 53.4 %copy-start = (bf16[1,1,512,768]{3,2,1,0:T(8,128)(2,1)S(1)}, bf16[1,1,512,768]{3,2,1,0:T(8,128)(2,1)}, u32[]{:S(2)}) copy-start(bf16[1,1,512,768]{3,2,1,0:T(8,128)(2,1)} %param.20) | copy-start | bytes 2359300
  175.2 9.5 copy-start.2
  175.2 9.5 copy-start.7
  187.2 171.7 %copy-start.1 = (f32[512,768]{1,0:T(8,128)}, f32[512,768]{1,0:T(8,128)S(1)}, u32[]{:S(2)}) copy-start(f32[512,768]{1,0:T(8,128)S(1)} %get-tuple-element.274) | copy-start | bytes 4718596
  187.5 161.9 %copy-start.4 = (bf16[1,1,512,768]{3,2,1,0:T(8,128)(2,1)S(1)}, bf16[1,1,512,768]{3,2,1,0:T(8,128)(2,1)}, u32[]{:S(2)}) copy-start(bf16[1,1,512,768]{3,2,1,0:T(8,128)(2,1)} %param.35) | copy-start | bytes 2359300
  349.5 9.4 copy-start.10
  358.8 3.0 copy-start.14
  363.9 1.3 copy-start.12
  364.2 0.9 copy-start.6
  471.9 21.7 %reduce-scatter.7.cloned.1.call-start = ((), (), s32[]{:S(2)}) async-start(), calls=%async_computation.10 | async-start | bytes 2359296 | tf_op jit(solution)/shard_map/reduce_scatter | solution.py:217
  472.7 125.3 %reduce-scatter.13.cloned.1.call-start = ((), (), s32[]{:S(2)}) async-start(), calls=%async_computation.13 | async-start | bytes 2433024 | tf_op jit(solution)/shard_map/reduce_scatter | solution.py:242
  476.3 246.7 %reduce-scatter.11.cloned.1.call-start = ((), (), s32[]{:S(2)}) async-start(), calls=%async_computation.12 | async-start | bytes 7299072 | tf_op jit(solution)/shard_map/reduce_scatter | solution.py:239
  500.2 363.8 %reduce-scatter.15.cloned.1.call-start = ((), (), s32[]{:S(2)}) async-start(), calls=%async_computation.14 | async-start | bytes 9732096 | tf_op jit(solution)/shard_map/reduce_scatter | solution.py:246
  509.2 496.8 %reduce-scatter.17.cloned.1.call-start = ((), (), s32[]{:S(2)}) async-start(), calls=%async_computation.15 | async-start | bytes 9732096 | tf_op jit(solution)/shard_map/reduce_scatter | solution.py:248
  520.2 9.8 copy-start.8
  520.2 10.0 copy-start.11
  520.2 10.0 copy-start.13
  532.5 1.2 copy-start.5
Sparse Core Ops, SparseCore 0:
  10.8 72.7 all-gather.8
  93.3 20.2 all-gather.16
  115.7 10.9 all-gather.18
  129.4 55.2 all-gather.10
  187.4 80.2 all-gather.12
  270.3 79.0 all-gather.14
  472.0 8.9 reduce-scatter.8
  483.3 10.2 reduce-scatter.6
  499.5 98.4 reduce-scatter.12
  605.0 118.0 reduce-scatter.10
  729.5 134.4 reduce-scatter.14
  871.3 134.5 reduce-scatter.16
where the time goes:
time: 1020 us; the launch traced here: 1010 us
  waiting for transfers between devices  631 us (62%)
  matrix products  207 us (20%)
  blocking collectives  106 us (10%)
  local copies, waits for them, and re-layouts  30.3 us (3%)
  other arithmetic  21 us (2%)
  between operations  16.4 us (2%)
    reduce_scatter x1, waiting for transfers between devices, body(): lax.psum_scatter(grad_proj, ('fsdp', 'ctx'), scatter_dimension=0, tiled=T...  142 us
    reduce_scatter x1, waiting for transfers between devices, body(): lax.psum_scatter(grad_fc, ('fsdp', 'ctx'), scatter_dimension=0, tiled=True)  141 us
    reduce_scatter x1, waiting for transfers between devices, body(): lax.psum_scatter(grad_qkv, ('fsdp', 'ctx'), scatter_dimension=0, tiled=True)  125 us
    unnamed x2, blocking collectives  106 us
    all_gather x1, waiting for transfers between devices, body(): lax.all_gather(w_fc, 'fsdp', axis=0, tiled=True)  80.2 us
    all_gather x1, waiting for transfers between devices, body(): lax.all_gather(w_proj, 'fsdp', axis=0, tiled=True)  74.8 us
    dot_general x4, matrix products, inner_rows(): lax.dot_general(left, right, (((0,), (0,)), ((), ())), preferred_element_...  29.5 us
    unnamed x62, local copies, waits for them, and re-layouts  23.9 us
  transfers between devices with their start and end apart: 12, of which 11 were waited for; matrix products, arithmetic and copies ran while one was open for 13% of the time, Pallas kernels for 0%

commit v1 on v0

--- a/solution.py
+++ b/solution.py
@@ -1,6 +1,10 @@
+import functools
+
 import jax
 import jax.numpy as jnp
 from jax import lax
+from jax.experimental import pallas as pl
+from jax.experimental.pallas import tpu as pltpu
 from jax.sharding import PartitionSpec as P
 
 HEADS = 12
@@ -50,6 +54,174 @@
     return lax.dot_general(
         left, right, (((1,), (1,)), ((), ())), preferred_element_type=jnp.float32
     )
+
+ROWS = 48
+LANES = 128
+VMEM_BYTES = 48 * 1024 * 1024
+
+
+def bits_of(count):
+    return count.bit_length() - 1
+
+
+def swap_chip(value, count, bit):
+    return lax.ppermute(value, "fsdp", [(i, i ^ (1 << bit)) for i in range(count)])
+
+
+def swap_core(value, count):
+    return lax.ppermute(value, "ctx", [(i, i ^ 1) for i in range(count)])
+
+
+def stage_orders(count):
+    nbits = bits_of(count)
+    high = list(range(nbits - 1, 1, -1))
+    return high, high + [0, 1], high + [1, 0]
+
+
+def mask_of(place, order):
+    return sum(((place >> k) & 1) << bit for k, bit in enumerate(order))
+
+
+def gather_pieces(shard, width_a, fsdp, n_ctx, core):
+    half = shard.shape[-1] // 2
+    high, order_a, order_b = stage_orders(fsdp)
+    held = lax.dynamic_slice_in_dim(shard, core * half, half, 2)
+    for bit in high:
+        held = jnp.concatenate([held, swap_chip(held, fsdp, bit)], axis=0)
+    part_a, part_b = held[..., :width_a], held[..., width_a:]
+    part_a = jnp.concatenate([part_a, swap_chip(part_a, fsdp, order_a[-2])], axis=0)
+    part_b = jnp.concatenate([part_b, swap_chip(part_b, fsdp, order_b[-2])], axis=0)
+    last_a = swap_chip(part_a, fsdp, order_a[-1])
+    last_b = swap_chip(part_b, fsdp, order_b[-1])
+    own = (part_a, last_a, part_b, last_b)
+    return own + tuple(swap_core(member, n_ctx) for member in own)
+
+
+def piece_moves(fsdp, half, width_a):
+    high, order_a, order_b = stage_orders(fsdp)
+    moves = []
+    for other in (0, 1):
+        for order, start, width in ((order_a, 0, width_a), (order_b, width_a, half - width_a)):
+            for first in (0, fsdp // 2):
+                moves.append((order, first, other, start, width))
+    return moves
+
+
+def assemble_kernel(fsdp, half, width_a, rows, column_blocks, index_ref, *refs):
+    pieces, whole = refs[:8], refs[8]
+    chip, core = index_ref[0], index_ref[1]
+    model = whole.shape[1]
+    for number, (order, first, other, start, width) in enumerate(piece_moves(fsdp, half, width_a)):
+        side = (1 - core) if other else core
+        column = side * half + start
+        for place in range(fsdp // 2):
+            origin = chip ^ mask_of(first + place, order)
+            if column_blocks == 1:
+                row, lane = origin * rows, pl.multiple_of(column, LANES)
+            else:
+                row, lane = (origin * column_blocks + column // model) * rows, 0
+            whole[pl.ds(pl.multiple_of(row, 16), rows), pl.ds(lane, width)] = pieces[number][place]
+
+
+def assemble(pieces, where, width_a, fsdp, column_blocks, model):
+    rows = pieces[0].shape[1]
+    half = width_a + pieces[2].shape[2]
+    shape = (fsdp * rows, 2 * half) if column_blocks == 1 else (fsdp * rows * column_blocks, model)
+    return pl.pallas_call(
+        functools.partial(assemble_kernel, fsdp, half, width_a, rows, column_blocks),
+        out_shape=jax.ShapeDtypeStruct(shape, pieces[0].dtype),
+        in_specs=[pl.BlockSpec(memory_space=pltpu.SMEM)] + [pl.BlockSpec(memory_space=pltpu.VMEM)] * 8,
+        out_specs=pl.BlockSpec(memory_space=pltpu.VMEM),
+        compiler_params=pltpu.CompilerParams(vmem_limit_bytes=VMEM_BYTES),
+    )(where, *pieces)
+
+
+def cut_kernel(fsdp, half, width_a, rows, column_blocks, index_ref, whole, *pieces):
+    chip, core = index_ref[0], index_ref[1]
+    high, order_a, order_b = stage_orders(fsdp)
+    model = whole.shape[1]
+    for number, (other, order, start, width) in enumerate(
+        (
+            (0, order_a, 0, width_a),
+            (0, order_b, width_a, half - width_a),
+            (1, order_a, 0, width_a),
+            (1, order_b, width_a, half - width_a),
+        )
+    ):
+        side = (1 - core) if other else core
+        column = side * half + start
+        for place in range(fsdp):
+            origin = chip ^ mask_of(place, order)
+            if column_blocks == 1:
+                row, lane = origin * rows, pl.multiple_of(column, LANES)
+            else:
+                row, lane = (origin * column_blocks + column // model) * rows, 0
+            block = whole[pl.ds(pl.multiple_of(row, 8), rows), pl.ds(lane, width)]
+            pieces[number][place] = block.astype(pieces[number].dtype)
+
+
+def cut(whole, where, rows, half, width_a, fsdp, column_blocks):
+    shapes = [(fsdp, rows, width_a), (fsdp, rows, half - width_a)] * 2
+    return pl.pallas_call(
+        functools.partial(cut_kernel, fsdp, half, width_a, rows, column_blocks),
+        out_shape=[jax.ShapeDtypeStruct(shape, jnp.bfloat16) for shape in shapes],
+        in_specs=[pl.BlockSpec(memory_space=pltpu.SMEM), pl.BlockSpec(memory_space=pltpu.VMEM)],
+        out_specs=[pl.BlockSpec(memory_space=pltpu.VMEM)] * 4,
+        compiler_params=pltpu.CompilerParams(vmem_limit_bytes=VMEM_BYTES),
+    )(where, whole)
+
+
+def add(left, right):
+    return left.astype(jnp.float32) + right.astype(jnp.float32)
+
+
+def scatter_pieces(pieces, fsdp, n_ctx):
+    keep_a, keep_b, send_a, send_b = pieces
+    high, order_a, order_b = stage_orders(fsdp)
+    low = jnp.bfloat16
+    sum_a = add(keep_a, swap_core(send_a, n_ctx)).astype(low)
+    sum_b = add(keep_b, swap_core(send_b, n_ctx)).astype(low)
+    for step in (-1, -2):
+        middle = sum_a.shape[0] // 2
+        got_a = swap_chip(sum_a[middle:], fsdp, order_a[step])
+        got_b = swap_chip(sum_b[middle:], fsdp, order_b[step])
+        sum_a = add(sum_a[:middle], got_a).astype(low)
+        sum_b = add(sum_b[:middle], got_b).astype(low)
+    total = jnp.concatenate([sum_a, sum_b], axis=2)
+    for bit in reversed(high):
+        middle = total.shape[0] // 2
+        got = swap_chip(total[middle:], fsdp, bit)
+        kept = total[:middle]
+        total = add(kept, got)
+        if middle > 1:
+            total = total.astype(low)
+    total = total[0]
+    if n_ctx > 2:
+        groups = [list(range(0, n_ctx, 2)), list(range(1, n_ctx, 2))]
+        total = lax.psum(total, "ctx", axis_index_groups=groups)
+    return total
+
+
+def share_rows(total, n_ctx, ctx_index):
+    rows = total.shape[0] // n_ctx
+    mine = lax.dynamic_slice_in_dim(total, ctx_index * rows, rows, 0)
+    theirs = swap_core(lax.dynamic_slice_in_dim(total, (ctx_index ^ 1) * rows, rows, 0), n_ctx)
+    first = (ctx_index & 1) == 0
+    return jnp.concatenate([jnp.where(first, mine, theirs), jnp.where(first, theirs, mine)], axis=1)
+
+
+def share_blocks(total, n_ctx, ctx_index, blocks):
+    rows = total.shape[0]
+    if n_ctx > 2:
+        theirs = swap_core(total, n_ctx)
+        first = (ctx_index & 1) == 0
+        total = jnp.concatenate([jnp.where(first, total, theirs), jnp.where(first, theirs, total)], axis=1)
+    parts = blocks if n_ctx > 2 else blocks // 2
+    stacked = jnp.moveaxis(total.reshape(rows, parts, -1), 1, 0).reshape(parts * rows, -1)
+    if n_ctx > 2:
+        count = stacked.shape[0] // n_ctx
+        stacked = lax.dynamic_slice_in_dim(stacked, ctx_index * count, count, 0)
+    return stacked
 
 
 def body(
@@ -74,36 +246,52 @@
     block_len = length // 2
     ctx_index = lax.axis_index("ctx")
     score_scale = HEAD_DIM ** (-0.5)
-    gathered = (
-        lax.all_gather(gain_one, "fsdp", axis=0, tiled=True),
-        lax.all_gather(bias_one, "fsdp", axis=0, tiled=True),
-        lax.all_gather(w_qkv, "fsdp", axis=0, tiled=True),
-        lax.all_gather(bias_q, "fsdp", axis=0, tiled=True),
-        lax.all_gather(bias_v, "fsdp", axis=0, tiled=True),
-        lax.all_gather(w_out, "fsdp", axis=0, tiled=True),
-        lax.all_gather(bias_out, "fsdp", axis=0, tiled=True),
-        lax.all_gather(gain_two, "fsdp", axis=0, tiled=True),
-        lax.all_gather(bias_two, "fsdp", axis=0, tiled=True),
-        lax.all_gather(w_fc, "fsdp", axis=0, tiled=True),
-        lax.all_gather(bias_fc, "fsdp", axis=0, tiled=True),
-        lax.all_gather(w_proj, "fsdp", axis=0, tiled=True),
-        lax.all_gather(bias_proj, "fsdp", axis=0, tiled=True),
-    )
+    fsdp = lax.axis_size("fsdp")
+    n_ctx = lax.axis_size("ctx")
+    core = ctx_index & 1
+    where = jnp.stack([lax.axis_index("fsdp"), core]).astype(jnp.int32)
+    rows = gain_one.shape[0]
+    small_rows = jnp.concatenate(
+        [
+            jnp.stack(
+                [gain_one, bias_one, bias_q, bias_v, bias_out, gain_two, bias_two, bias_proj], axis=1
+            ),
+            bias_fc.reshape(-1, rows).T,
+        ],
+        axis=1,
+    )
+    small_count = small_rows.shape[1]
+    small_rows = jnp.pad(small_rows, ((0, 0), (0, 2 * LANES - small_count)))
+    width_one, width_two, width_three = 640, 1024, 768
+    model_full = fsdp * rows
+    blocks = w_proj.shape[0] // rows
+    group_one = jnp.concatenate([w_qkv, small_rows], axis=1)[None]
+    group_two = jnp.concatenate([w_fc, w_out], axis=1)[None]
+    group_three = jnp.moveaxis(w_proj.reshape(blocks, rows, model_full), 0, 1).reshape(1, rows, -1)
+    whole_one = assemble(
+        gather_pieces(group_one, width_one, fsdp, n_ctx, core), where, width_one, fsdp, 1, model_full
+    )
+    whole_two = assemble(
+        gather_pieces(group_two, width_two, fsdp, n_ctx, core), where, width_two, fsdp, 1, model_full
+    )
+    proj_full = assemble(
+        gather_pieces(group_three, width_three, fsdp, n_ctx, core), where, width_three, fsdp, blocks, model_full
+    )
+    qkv_full = whole_one[:, : 3 * model_full]
+    fc_full = whole_two[:, : w_fc.shape[1]]
+    out_full = whole_two[:, w_fc.shape[1] :]
+    small_full = whole_one[:, 3 * model_full : 3 * model_full + small_count].T.astype(jnp.float32)
     (
         gain_first,
         bias_first,
-        qkv_full,
         query_bias,
         value_bias,
-        out_full,
         out_bias,
         gain_second,
         bias_second,
-        fc_full,
-        fc_bias,
-        proj_full,
         proj_bias,
-    ) = [member.astype(jnp.float32) if member.ndim == 1 else member for member in gathered]
+    ) = [small_full[i] for i in range(8)]
+    fc_bias = jnp.moveaxis(small_full[8:].reshape(blocks, fsdp, rows), 0, 1).reshape(-1)
     flat_rows = tokens.astype(jnp.float32).reshape(seq_count * length, model_width)
     norm_first, pull_first = jax.vjp(layer_norm, flat_rows, gain_first, bias_first)
     normed = norm_first.astype(jnp.bfloat16)
@@ -233,36 +421,49 @@
     d_normed = times_t(d_qkv, qkv_full)
     d_rows_norm, grad_gain_first, grad_bias_first = pull_first(d_normed)
     grad_inputs = (d_middle + d_rows_norm).reshape(tokens.shape)
-    shares = (
-        lax.psum_scatter(grad_gain_first, ("fsdp", "ctx"), scatter_dimension=0, tiled=True),
-        lax.psum_scatter(grad_bias_first, ("fsdp", "ctx"), scatter_dimension=0, tiled=True),
-        lax.psum_scatter(grad_qkv, ("fsdp", "ctx"), scatter_dimension=0, tiled=True),
-        lax.psum_scatter(sum_query_bias, ("fsdp", "ctx"), scatter_dimension=0, tiled=True),
-        lax.psum_scatter(sum_value_bias, ("fsdp", "ctx"), scatter_dimension=0, tiled=True),
-        lax.psum_scatter(grad_out_w, ("fsdp", "ctx"), scatter_dimension=0, tiled=True),
-        lax.psum_scatter(sum_out_bias, ("fsdp", "ctx"), scatter_dimension=0, tiled=True),
-        lax.psum_scatter(grad_gain_second, ("fsdp", "ctx"), scatter_dimension=0, tiled=True),
-        lax.psum_scatter(grad_bias_second, ("fsdp", "ctx"), scatter_dimension=0, tiled=True),
-        lax.psum_scatter(grad_fc, ("fsdp", "ctx"), scatter_dimension=0, tiled=True),
-        lax.psum_scatter(sum_fc_bias, ("fsdp", "ctx"), scatter_dimension=0, tiled=True),
-        lax.psum_scatter(grad_proj, ("fsdp", "ctx"), scatter_dimension=0, tiled=True),
-        lax.psum_scatter(sum_proj_bias, ("fsdp", "ctx"), scatter_dimension=0, tiled=True),
-    )
+    low = jnp.bfloat16
+    sums_fc = jnp.moveaxis(sum_fc_bias.reshape(fsdp, n_ctx, blocks, rows // n_ctx), 2, 0).reshape(blocks, -1)
+    small_sums = jnp.concatenate(
+        [
+            jnp.stack(
+                [
+                    grad_gain_first,
+                    grad_bias_first,
+                    sum_query_bias,
+                    sum_value_bias,
+                    sum_out_bias,
+                    grad_gain_second,
+                    grad_bias_second,
+                    sum_proj_bias,
+                ]
+            ),
+            sums_fc,
+        ]
+    )
+    small_sums = jnp.pad(small_sums, ((0, 2 * LANES - small_count), (0, 0))).T
+    grads_one = jnp.concatenate([grad_qkv.astype(low), small_sums.astype(low)], axis=1)
+    grads_two = jnp.concatenate([grad_fc.astype(low), grad_out_w.astype(low)], axis=1)
+    parts_three = cut(grad_proj.astype(low), where, rows, blocks * model_full // 2, width_three, fsdp, blocks)
+    parts_two = cut(grads_two, where, rows, grads_two.shape[1] // 2, width_two, fsdp, 1)
+    parts_one = cut(grads_one, where, rows, grads_one.shape[1] // 2, width_one, fsdp, 1)
+    share_proj = share_blocks(scatter_pieces(parts_three, fsdp, n_ctx), n_ctx, ctx_index, blocks)
+    share_two = share_rows(scatter_pieces(parts_two, fsdp, n_ctx), n_ctx, ctx_index)
+    share_one = share_rows(scatter_pieces(parts_one, fsdp, n_ctx), n_ctx, ctx_index)
+    share_qkv = share_one[:, : 3 * model_width]
+    share_fc = share_two[:, : w_fc.shape[1]]
+    share_out = share_two[:, w_fc.shape[1] :]
+    small_share = share_one[:, 3 * model_width : 3 * model_width + small_count].T
     (
         share_gain_one,
         share_bias_one,
-        share_qkv,
         share_bias_q,
         share_bias_v,
-        share_out,
         share_bias_out,
         share_gain_two,
         share_bias_two,
-        share_fc,
-        share_bias_fc,
-        share_proj,
         share_bias_proj,
-    ) = shares
+    ) = [small_share[i] for i in range(8)]
+    share_bias_fc = small_share[8:].reshape(-1)
     return (
         out_tokens,
         grad_inputs,

time: 1020 us -> 502 us (0.49)
  waiting for transfers between devices: 631 us -> 89.6 us
  blocking collectives: 106 us -> 0 us
  starting transfers between devices: 0.9 us -> 69.7 us
  other arithmetic: 21 us -> 52.9 us
  Pallas kernels: 0 us -> 24.8 us
  local copies, waits for them, and re-layouts: 30.3 us -> 47.3 us
  matrix products: 207 us -> 192 us
    reduce_scatter x4 -> x0, waiting for transfers between devices: 424 us -> none  [the longest x1 142 us: body(): lax.psum_scatter(grad_proj, ('fsdp', 'ctx'), scatter_dimension=0, tiled=T...]
    all_gather x4 -> x0, waiting for transfers between devices: 164 us -> none  [the longest x1 80.2 us: body(): lax.all_gather(w_fc, 'fsdp', axis=0, tiled=True)]
    unnamed x2 -> x0, blocking collectives: 106 us -> none
    ppermute x0 -> x56, waiting for transfers between devices: none -> 89.5 us  [the longest x36 88.6 us: swap_chip(): lax.ppermute(value, 'fsdp', [(i, i ^ 1 << bit) for i in range(count)])]
    ppermute x0 -> x56, starting transfers between devices: none -> 69.1 us  [the longest x36 35.1 us: swap_chip(): lax.ppermute(value, 'fsdp', [(i, i ^ 1 << bit) for i in range(count)])]
    pallas_call x0 -> x6, Pallas kernels: none -> 24.8 us  [the longest x3 12.5 us: cut(): pl.pallas_call(functools.partial(cut_kernel, fsdp, half, width_a, rows, c...]
    concatenate x0 -> x19, other arithmetic: none -> 15.3 us  [the longest x1 5.26 us: body(): jnp.concatenate([grad_fc.astype(low), grad_out_w.astype(low)], axis=1)]
    convert_element_type x9 -> x22, other arithmetic: 0.03 us -> 15.2 us  [the longest x3 5.18 us: scatter_pieces(): sum_b = add(keep_b, swap_core(send_b, n_ctx)).astype(low)]
  transfers between devices with their start and end apart: 12 -> 60, of which waited for: 11 -> 20; matrix products, arithmetic and copies ran while one was open for 13% -> 20% of each run, Pallas kernels for 0% -> 5%
where the time goes in v1:
time: 502 us; the launch traced here: 492 us
  matrix products  192 us (38%)
  waiting for transfers between devices  89.6 us (18%)
  starting transfers between devices  69.7 us (14%)
  other arithmetic  52.9 us (11%)
  local copies, waits for them, and re-layouts  47.3 us (9%)
  Pallas kernels  24.8 us (5%)
  between operations  15.4 us (3%)
    ppermute x36, waiting for transfers between devices, swap_chip(): lax.ppermute(value, 'fsdp', [(i, i ^ 1 << bit) for i in range(count)])  88.6 us
    ppermute x36, starting transfers between devices, swap_chip(): lax.ppermute(value, 'fsdp', [(i, i ^ 1 << bit) for i in range(count)])  35.1 us
    ppermute x20, starting transfers between devices, swap_core(): return lax.ppermute(value, 'ctx', [(i, i ^ 1) for i in range(count)])  34 us
    dot_general x12, matrix products, head_back_keys(): jnp.einsum('sqk,sqd->skd', d_scores, query_h, preferred_element_type=jnp....  22.9 us
    dot_general x12, matrix products, score_grads(): jnp.einsum('sqd,skd->sqk', query_h, key_h, preferred_element_type=jnp.flo...  22.5 us
    unnamed x107, local copies, waits for them, and re-layouts  22.3 us
    dot_general x12, matrix products, head_back_keys(): jnp.einsum('sqk,sqd->skd', prob_full.astype(jnp.bfloat16), dmix_h, prefer...  21.4 us
    dot_general x12, matrix products, head_forward(): jnp.einsum('sqd,skd->sqk', query_h, key_h, preferred_element_type=jnp.flo...  18.9 us
  transfers between devices with their start and end apart: 60, of which 20 were waited for; matrix products, arithmetic and copies ran while one was open for 20% of the time, Pallas kernels for 5%

profile of v1, /device:TPU:1, one launch (start us, length us, event | category | flops | bytes accessed | tf_op | source)
XLA Modules:
  0.0 492.2 jit_solution(2448597240229794661)
XLA Ops:
  9.9 3.2 collective-permute-start
  13.1 5.7 %collective-permute-done = bf16[1,48,1280]{2,1,0:T(8,128)(2,1)S(1)} collective-permute-done((bf16[1,48,1280]{2,1,0:T(8,128)(2,1)S(1)}, bf16[1,48,1280]{2,1,0:T(8,128)(2,1)S(1)}, u32[]{:S(2)}, u32[]{:S(2)}) %collective-permute-start) | collective-permute-done | bytes 122912 | tf_op jit(solution)/shard_map/ppermute | solution.py:68
  21.4 3.7 collective-permute-done.1
  27.0 4.2 collective-permute-start.20
  32.9 4.2 collective-permute-done.4
  38.7 4.8 collective-permute-start.6
  43.4 4.1 collective-permute-done.3.refs_1_
  47.6 2.5 collective-permute-start.7
  53.9 3.3 shard_map.271
  60.8 4.2 fusion.56
  65.0 2.1 copy-done.21
  72.5 6.4 %collective-permute-done.11 = bf16[2,48,1920]{2,1,0:T(8,128)(2,1)S(1)} collective-permute-done((bf16[2,48,1920]{2,1,0:T(8,128)(2,1)S(1)}, bf16[2,48,1920]{2,1,0:T(8,128)(2,1)S(1)}, u32[]{:S(2)}, u32[]{:S(2)}) %collective-permute-start.11) | collective-permute-done | bytes 368672 | tf_op jit(solution)/shard_map/ppermute | solution.py:68
  84.4 5.1 %collective-permute-done.12 = bf16[4,48,1024]{2,1,0:T(8,128)(2,1)S(1)} collective-permute-done((bf16[4,48,1024]{2,1,0:T(8,128)(2,1)S(1)}, bf16[4,48,1024]{2,1,0:T(8,128)(2,1)S(1)}, u32[]{:S(2)}, u32[]{:S(2)}) %collective-permute-start.12) | collective-permute-done | bytes 393248 | tf_op jit(solution)/shard_map/ppermute | solution.py:68
  92.9 4.2 collective-permute-start.26
  98.6 3.9 collective-permute-done.23.refs_1_
  102.5 4.8 collective-permute-start.28
  108.7 10.6 %collective-permute-done.13.refs_1_ = bf16[8,48,1024]{2,1,0:T(8,128)(2,1)S(1)} collective-permute-done((bf16[8,48,1024]{2,1,0:T(8,128)(2,1)S(1)}, bf16[8,48,1024]{2,1,0:T(8,128)(2,1)S(1)}, u32[]{:S(2)}, u32[]{:S(2)}) %collective-permute-start.13) | collective-permute-done | bytes 786464 | tf_op jit(solution)/shard_map/ppermute | solution.py:68
  119.2 2.6 collective-permute-start.17
  124.8 1.9 slice.302
  126.8 2.3 copy.95
  129.1 2.4 copy.99
  134.9 4.1 shard_map.273
  139.0 5.0 %shard_map.272 = bf16[768,3840]{1,0:T(8,128)(2,1)} custom-call(s32[2]{0:T(128)S(1)} %pad_add_fusion.index_ref, bf16[8,48,1024]{2,1,0:T(8,128)(2,1)S(1)} %pad_maximum_fusion.2.refs_0_, bf16[8,48,1024]{2,1,0:T(8,128)(2,1)S(1)} %collective-permute-done.13.refs_1_, bf16[8,48,896]{2,1,0:T(8,128)(2,1)S(1)} %pad_maximum_fusion.4.refs_2_, ...), custom_call_target="tpu_custom_call" | custom-call | tf_op jit(solution)/shard_map/pallas_call | solution.py:130
  145.7 2.7 copy.100
  150.1 2.8 copy.101
  153.0 44.0 %while.28 = (s32[]{:T(128)}, bf16[12,1,512,64]{2,3,1,0:T(8,128)(2,1)S(1)}, f32[12,1,512]{2,1,0:T(1,128)S(1)}, bf16[12,1,512,64]{3,2,1,0:T(8,128)(2,1)}, bf16[12,...) while((s32[]{:T(128)}, ...), condition=%wide.region_5.6_spmd.clone, body=%wide.region_2.5_spmd.clone.sunk | while | flops 138935808 | bytes 7106665 | solution.py:339
  197.0 2.5 fusion.115
  199.9 5.5 %fusion.52 = f32[512,3072]{1,0:T(8,128)S(1)} fusion(bf16[768,3840]{1,0:T(8,128)(2,1)} %shard_map.272, f32[512,768]{1,0:T(8,128)S(1)} %get-tuple-element.321, f32[768]{0:T(1024)S(1)} %copy-done.39, f32[768]{0:T(1024)S(1)} %get-tuple-element.246, f32[512]{0:T(512)S(1)} %fusion.103, f32[512]{0:T(512)S(1)} %broadcast_multiply_fusion), kind=kOutput, calls=%fused_computation.72 | convolution fusion | flops 2417885184 | bytes 12593152 | tf_op jit(solution)/shard_map/dot_general | solution.py:345
  205.4 6.7 %fusion.116 = (bf16[3072]{0:T(1024)(128)(2,1)S(1)}, bf16[512,3072]{1,0:T(8,128)(2,1)S(1)}) fusion(f32[512,3072]{1,0:T(8,128)S(1)} %fusion.52, f32[3072]{0:T(1024)S(1)} %add.293, bf16[3072,768]{1,0:T(8,128)(2,1)S(1)} %bitcast.252, bf16[1,1,512,768]{3,2,1,0:T(8,128)(2,1)S(1)} %copy-done.15), kind=kOutput, calls=%fused_computation.245 | convolution fusion | flops 2450519040 | bytes 14960640 | tf_op jit(solution)/shard_map/dot_general | solution.py:54
  212.2 2.9 multiply_reduce_fusion.1
  220.2 104.5 %while.29 = (s32[]{:T(128)}, bf16[12,1,512,64]{2,3,1,0:T(8,128)(2,1)S(1)}, bf16[12,1,1024,64]{2,3,1,0:T(8,128)(2,1)}, bf16[12,1,1024,64]{2,3,1,0:T(8,128)(2,1)},...) while((s32[]{:T(128)}, ...), condition=%wide.region_12.13_spmd.clone, body=%wide.region_10.12_spmd.clone.sunk | while | flops 340884992 | bytes 17585280 | solution.py:401
  225.2 1.9 fusion.157
  242.6 1.9 fusion.157
  251.3 1.9 fusion.157
  260.1 1.9 fusion.157
  268.8 1.9 fusion.157
  277.5 1.9 fusion.157
  286.2 1.9 fusion.157
  294.9 1.9 fusion.157
  303.6 1.9 fusion.157
  312.3 1.9 fusion.157
  321.0 1.9 fusion.157
  324.8 8.9 %convolution_convert_fusion.whole = bf16[3072,768]{1,0:T(8,128)(2,1)} fusion(bf16[1,1,512,768]{3,2,1,0:T(8,128)(2,1)S(1)} %copy-done.15, f32[512,3072]{1,0:T(8,128)} %copy-done.42, f32[3072]{0:T(1024)S(1)} %add.293), kind=kOutput, calls=%fused_computation.67 | convolution fusion | flops 2434007040 | bytes 11808768 | tf_op jit(solution)/shard_map/dot_general | solution.py:48
  333.8 4.2 shard_map.276
  341.9 5.0 %convolution_convert_fusion.1 = bf16[768,3072]{1,0:T(8,128)(2,1)} fusion(bf16[512,3072]{1,0:T(8,128)(2,1)S(1)} %copy-done.44, f32[512,768]{1,0:T(8,128)S(1)} %get-tuple-element.321, f32[768]{0:T(1024)S(1)} %copy-done.39, f32[768]{0:T(1024)S(1)} %get-tuple-element.246, f32[512]{0:T(512)S(1)} %fusion.103, f32[512]{0:T(512)S(1)} %broadcast_multiply_fusion), kind=kOutput, calls=%fused_computation.68 | convolution fusion | flops 2420244480 | bytes 9447424 | tf_op jit(solution)/shard_map/dot_general | solution.py:48
  346.9 5.3 %pad_maximum_fusion.whole = bf16[768,3840]{1,0:T(8,128)(2,1)} fusion(bf16[768,768]{1,0:T(8,128)(2,1)S(1)} %convolution_convert_fusion.3, bf16[768,3072]{1,0:T(8,128)(2,1)} %convolution_convert_fusion.1), kind=kLoop, calls=%fused_computation.66 | loop fusion | flops 11796480 | bytes 11796480 | tf_op jit(solution)/shard_map/concatenate | solution.py:445
  352.2 4.8 shard_map.275
  357.9 7.6 %fusion.77 = bf16[1,1,512,768]{3,2,1,0:T(8,128)(2,1)} fusion(f32[512,768]{1,0:T(8,128)S(1)} %copy-done.18, bf16[3072,768]{1,0:T(8,128)(2,1)S(1)} %bitcast.254, f32[768]{0:T(1024)S(1)} %get-tuple-element.247, f32[512,3072]{1,0:T(8,128)} %copy-done.42, f32[3072]{0:T(1024)S(1)} %add.293), kind=kOutput, calls=%fused_computation.124 | convolution fusion | flops 2432827392 | bytes 13384704 | tf_op jit(solution)/shard_map/dot_general | solution.py:349
  367.3 2.0 add_convert_fusion.2
  375.4 8.9 %collective-permute-done.52 = bf16[8,48,768]{2,1,0:T(8,128)(2,1)S(1)} collective-permute-done((bf16[8,48,768]{2,1,0:T(8,128)(2,1)S(1)}, bf16[8,48,768]{2,1,0:T(8,128)(2,1)S(1)}, u32[]{:S(2)}, u32[]{:S(2)}) %collective-permute-start.52) | collective-permute-done | bytes 589856 | tf_op jit(solution)/shard_map/ppermute | solution.py:68
  387.4 2.1 add_convert_fusion
  391.9 13.5 %collective-permute-done.50 = bf16[4,48,768]{2,1,0:T(8,128)(2,1)S(1)} collective-permute-done((bf16[4,48,768]{2,1,0:T(8,128)(2,1)S(1)}, bf16[4,48,768]{2,1,0:T(8,128)(2,1)S(1)}, u32[]{:S(2)}, u32[]{:S(2)}) %collective-permute-start.50) | collective-permute-done | bytes 294944 | tf_op jit(solution)/shard_map/ppermute | solution.py:68
  407.2 2.0 collective-permute-done.40
  416.0 4.8 fusion.108
  423.6 3.5 convolution_convert_fusion.2
  427.1 2.2 pad_maximum_fusion.1.whole
  429.3 3.5 shard_map.274
  432.7 2.4 collective-permute-start.33
  448.6 4.0 collective-permute-done.45
  452.9 3.6 collective-permute-done.34
  461.4 3.2 collective-permute-done.35
  466.1 3.9 collective-permute-start.47
  471.1 5.0 %collective-permute-done.37 = bf16[1,48,1280]{2,1,0:T(8,128)(2,1)S(1)} collective-permute-done((bf16[1,48,1280]{2,1,0:T(8,128)(2,1)S(1)}, bf16[1,48,1280]{2,1,0:T(8,128)(2,1)S(1)}, u32[]{:S(2)}, u32[]{:S(2)}) %collective-permute-start.37) | collective-permute-done | bytes 122912 | tf_op jit(solution)/shard_map/ppermute | solution.py:68
  476.2 5.3 %collective-permute-start.38 = (f32[24,1280]{1,0:T(8,128)S(1)}, f32[24,1280]{1,0:T(8,128)S(1)}, u32[]{:S(2)}, u32[]{:S(2)}) collective-permute-start(f32[24,1280]{1,0:T(8,128)S(1)} %dynamic-slice_bitcast_fusion.1), channel_id=1, source_target_pairs={{0,1},{1,0},{2,3},{3,2},{4,5},{5,4},{6,7},{7,6},{8,9},{9,8},{10,11... | collective-permute-start | bytes 368648 | tf_op jit(solution)/shard_map/ppermute | solution.py:72
  (470 shorter events, 231.0 us)
Async XLA Ops:
  7.2 136.8 %all-gather.5.cloned.1.call-start = ((), (), s32[]{:S(2)}) async-start(), calls=%async_computation.4 | async-start | bytes 2359296 | tf_op jit(solution)/shard_map/all_gather | solution.py:315
  9.9 8.9 %collective-permute-start = (bf16[1,48,1280]{2,1,0:T(8,128)(2,1)S(1)}, bf16[1,48,1280]{2,1,0:T(8,128)(2,1)S(1)}, u32[]{:S(2)}, u32[]{:S(2)}) collective-permute-start(bf16[1,48,1280]{2,1,0:T(8,128)(2,1)S(1)} %fusion.101), channel_id=1, source_target_pairs={{0,16},{2,18},{4,20},{6,22},{8,24},{10,26},{12,28},{14,30},{16,0},... | collective-permute-start | bytes 368648 | tf_op jit(solution)/shard_map/ppermute | solution.py:68
  18.8 6.3 %collective-permute-start.1 = (bf16[2,48,1280]{2,1,0:T(8,128)(2,1)S(1)}, bf16[2,48,1280]{2,1,0:T(8,128)(2,1)S(1)}, u32[]{:S(2)}, u32[]{:S(2)}) collective-permute-start(bf16[2,48,1280]{2,1,0:T(8,128)(2,1)S(1)} %pad_maximum_fusion.18), channel_id=1, source_target_pairs={{0,8},{2,10},{4,12},{6,14},{8,0},{10,2},{12,4},{14,6},{16,24},{18,... | collective-permute-start | bytes 737288 | tf_op jit(solution)/shard_map/ppermute | solution.py:68
  25.2 7.3 %collective-permute-start.2 = (bf16[4,48,640]{2,1,0:T(8,128)(2,1)S(1)}, bf16[4,48,640]{2,1,0:T(8,128)(2,1)S(1)}, u32[]{:S(2)}, u32[]{:S(2)}) collective-permute-start(bf16[4,48,640]{2,1,0:T(8,128)(2,1)S(1)} %get-tuple-element.315), channel_id=1, source_target_pairs={{0,2},{2,0},{4,6},{6,4},{8,10},{10,8},{12,14},{14,12},{16,18},{18,... | collective-permute-start | bytes 737288 | tf_op jit(solution)/shard_map/ppermute | solution.py:68
  27.0 24.0 %collective-permute-start.20 = (bf16[1,48,1536]{2,1,0:T(8,128)(2,1)}, bf16[1,48,1536]{2,1,0:T(8,128)(2,1)}, u32[]{:S(2)}, u32[]{:S(2)}) collective-permute-start(bf16[1,48,1536]{2,1,0:T(8,128)(2,1)} %constant_dynamic-slice_fusion.1), channel_id=1, source_target_pairs={{0,16},{2,18},{4,20},{6,22},{8,24},{10,26},{12,28},{14,30},{16,0},... | collective-permute-start | bytes 442376 | tf_op jit(solution)/shard_map/ppermute | solution.py:68
  31.2 6.0 %collective-permute-start.4 = (bf16[4,48,640]{2,1,0:T(8,128)(2,1)S(1)}, bf16[4,48,640]{2,1,0:T(8,128)(2,1)S(1)}, u32[]{:S(2)}, u32[]{:S(2)}) collective-permute-start(bf16[4,48,640]{2,1,0:T(8,128)(2,1)S(1)} %get-tuple-element.314), channel_id=1, source_target_pairs={{0,4},{2,6},{4,0},{6,2},{8,12},{10,14},{12,8},{14,10},{16,20},{18,... | collective-permute-start | bytes 737288 | tf_op jit(solution)/shard_map/ppermute | solution.py:68
  32.7 14.9 %collective-permute-start.3 = (bf16[8,48,640]{2,1,0:T(8,128)(2,1)S(1)}, bf16[8,48,640]{2,1,0:T(8,128)(2,1)S(1)}, u32[]{:S(2)}, u32[]{:S(2)}) collective-permute-start(bf16[8,48,640]{2,1,0:T(8,128)(2,1)S(1)} %pad_maximum_fusion.9.refs_0_), channel_id=1, source_target_pairs={{0,4},{2,6},{4,0},{6,2},{8,12},{10,14},{12,8},{14,10},{16,20},{18,... | collective-permute-start | bytes 1474568 | tf_op jit(solution)/shard_map/ppermute | solution.py:68
  37.2 12.9 %collective-permute-start.5 = (bf16[8,48,640]{2,1,0:T(8,128)(2,1)S(1)}, bf16[8,48,640]{2,1,0:T(8,128)(2,1)S(1)}, u32[]{:S(2)}, u32[]{:S(2)}) collective-permute-start(bf16[8,48,640]{2,1,0:T(8,128)(2,1)S(1)} %pad_maximum_fusion.10.refs_2_), channel_id=1, source_target_pairs={{0,2},{2,0},{4,6},{6,4},{8,10},{10,8},{12,14},{14,12},{16,18},{18,... | collective-permute-start | bytes 1474568 | tf_op jit(solution)/shard_map/ppermute | solution.py:68
  38.7 14.3 %collective-permute-start.6 = (bf16[8,48,640]{2,1,0:T(8,128)(2,1)S(1)}, bf16[8,48,640]{2,1,0:T(8,128)(2,1)S(1)}, u32[]{:S(2)}, u32[]{:S(2)}) collective-permute-start(bf16[8,48,640]{2,1,0:T(8,128)(2,1)S(1)} %pad_maximum_fusion.9.refs_0_), channel_id=1, source_target_pairs={{0,1},{1,0},{2,3},{3,2},{4,5},{5,4},{6,7},{7,6},{8,9},{9,8},{10,11... | collective-permute-start | bytes 1474568 | tf_op jit(solution)/shard_map/ppermute | solution.py:72
  43.4 10.4 %collective-permute-start.8 = (bf16[8,48,640]{2,1,0:T(8,128)(2,1)S(1)}, bf16[8,48,640]{2,1,0:T(8,128)(2,1)S(1)}, u32[]{:S(2)}, u32[]{:S(2)}) collective-permute-start(bf16[8,48,640]{2,1,0:T(8,128)(2,1)S(1)} %pad_maximum_fusion.10.refs_2_), channel_id=1, source_target_pairs={{0,1},{1,0},{2,3},{3,2},{4,5},{5,4},{6,7},{7,6},{8,9},{9,8},{10,11... | collective-permute-start | bytes 1474568 | tf_op jit(solution)/shard_map/ppermute | solution.py:72
  47.6 6.3 %collective-permute-start.7 = (bf16[8,48,640]{2,1,0:T(8,128)(2,1)S(1)}, bf16[8,48,640]{2,1,0:T(8,128)(2,1)S(1)}, u32[]{:S(2)}, u32[]{:S(2)}) collective-permute-start(bf16[8,48,640]{2,1,0:T(8,128)(2,1)S(1)} %collective-permute-done.3.refs_1_), channel_id=1, source_target_pairs={{0,1},{1,0},{2,3},{3,2},{4,5},{5,4},{6,7},{7,6},{8,9},{9,8},{10,11... | collective-permute-start | bytes 1474568 | tf_op jit(solution)/shard_map/ppermute | solution.py:72
  50.1 3.8 collective-permute-start.9
  51.0 17.2 %collective-permute-start.10 = (bf16[1,48,1920]{2,1,0:T(8,128)(2,1)}, bf16[1,48,1920]{2,1,0:T(8,128)(2,1)}, u32[]{:S(2)}, u32[]{:S(2)}) collective-permute-start(bf16[1,48,1920]{2,1,0:T(8,128)(2,1)} %fusion.99), channel_id=1, source_target_pairs={{0,16},{2,18},{4,20},{6,22},{8,24},{10,26},{12,28},{14,30},{16,0},... | collective-permute-start | bytes 552968 | tf_op jit(solution)/shard_map/ppermute | solution.py:68
  53.0 16.8 %collective-permute-start.21 = (bf16[2,48,1536]{2,1,0:T(8,128)(2,1)}, bf16[2,48,1536]{2,1,0:T(8,128)(2,1)}, u32[]{:S(2)}, u32[]{:S(2)}) collective-permute-start(bf16[2,48,1536]{2,1,0:T(8,128)(2,1)} %pad_maximum_fusion.16), channel_id=1, source_target_pairs={{0,8},{2,10},{4,12},{6,14},{8,0},{10,2},{12,4},{14,6},{16,24},{18,... | collective-permute-start | bytes 884744 | tf_op jit(solution)/shard_map/ppermute | solution.py:68
  68.1 80.3 %all-gather.7.cloned.1.call-start = ((), (), s32[]{:S(2)}) async-start(), calls=%async_computation.5 | async-start | bytes 2359296 | tf_op jit(solution)/shard_map/all_gather | solution.py:316
  69.2 9.8 %collective-permute-start.11 = (bf16[2,48,1920]{2,1,0:T(8,128)(2,1)S(1)}, bf16[2,48,1920]{2,1,0:T(8,128)(2,1)S(1)}, u32[]{:S(2)}, u32[]{:S(2)}) collective-permute-start(bf16[2,48,1920]{2,1,0:T(8,128)(2,1)S(1)} %pad_maximum_fusion.12), channel_id=1, source_target_pairs={{0,8},{2,10},{4,12},{6,14},{8,0},{10,2},{12,4},{14,6},{16,24},{18,... | collective-permute-start | bytes 1105928 | tf_op jit(solution)/shard_map/ppermute | solution.py:68
  71.0 11.7 %collective-permute-start.22 = (bf16[4,48,768]{2,1,0:T(8,128)(2,1)S(1)}, bf16[4,48,768]{2,1,0:T(8,128)(2,1)S(1)}, u32[]{:S(2)}, u32[]{:S(2)}) collective-permute-start(bf16[4,48,768]{2,1,0:T(8,128)(2,1)S(1)} %get-tuple-element.311), channel_id=1, source_target_pairs={{0,2},{2,0},{4,6},{6,4},{8,10},{10,8},{12,14},{14,12},{16,18},{18,... | collective-permute-start | bytes 884744 | tf_op jit(solution)/shard_map/ppermute | solution.py:68
  71.9 11.6 %collective-permute-start.24 = (bf16[4,48,768]{2,1,0:T(8,128)(2,1)S(1)}, bf16[4,48,768]{2,1,0:T(8,128)(2,1)S(1)}, u32[]{:S(2)}, u32[]{:S(2)}) collective-permute-start(bf16[4,48,768]{2,1,0:T(8,128)(2,1)S(1)} %get-tuple-element.310), channel_id=1, source_target_pairs={{0,4},{2,6},{4,0},{6,2},{8,12},{10,14},{12,8},{14,10},{16,20},{18,... | collective-permute-start | bytes 884744 | tf_op jit(solution)/shard_map/ppermute | solution.py:68
  80.0 9.5 %collective-permute-start.12 = (bf16[4,48,1024]{2,1,0:T(8,128)(2,1)S(1)}, bf16[4,48,1024]{2,1,0:T(8,128)(2,1)S(1)}, u32[]{:S(2)}, u32[]{:S(2)}) collective-permute-start(bf16[4,48,1024]{2,1,0:T(8,128)(2,1)S(1)} %slice.296), channel_id=1, source_target_pairs={{0,2},{2,0},{4,6},{6,4},{8,10},{10,8},{12,14},{14,12},{16,18},{18,... | collective-permute-start | bytes 1179656 | tf_op jit(solution)/shard_map/ppermute | solution.py:68
  81.8 15.3 %collective-permute-start.14 = (bf16[4,48,896]{2,1,0:T(8,128)(2,1)S(1)}, bf16[4,48,896]{2,1,0:T(8,128)(2,1)}, u32[]{:S(2)}, u32[]{:S(2)}) collective-permute-start(bf16[4,48,896]{2,1,0:T(8,128)(2,1)S(1)} %pad_maximum_fusion.13), channel_id=1, source_target_pairs={{0,4},{2,6},{4,0},{6,2},{8,12},{10,14},{12,8},{14,10},{16,20},{18,... | collective-permute-start | bytes 1032200 | tf_op jit(solution)/shard_map/ppermute | solution.py:68
  82.8 19.7 %collective-permute-start.23 = (bf16[8,48,768]{2,1,0:T(8,128)(2,1)S(1)}, bf16[8,48,768]{2,1,0:T(8,128)(2,1)}, u32[]{:S(2)}, u32[]{:S(2)}) collective-permute-start(bf16[8,48,768]{2,1,0:T(8,128)(2,1)S(1)} %pad_maximum_fusion.6.refs_0_), channel_id=1, source_target_pairs={{0,4},{2,6},{4,0},{6,2},{8,12},{10,14},{12,8},{14,10},{16,20},{18,... | collective-permute-start | bytes 1769480 | tf_op jit(solution)/shard_map/ppermute | solution.py:68
  83.5 23.8 %collective-permute-start.25 = (bf16[8,48,768]{2,1,0:T(8,128)(2,1)S(1)}, bf16[8,48,768]{2,1,0:T(8,128)(2,1)}, u32[]{:S(2)}, u32[]{:S(2)}) collective-permute-start(bf16[8,48,768]{2,1,0:T(8,128)(2,1)S(1)} %pad_maximum_fusion.7.refs_2_), channel_id=1, source_target_pairs={{0,2},{2,0},{4,6},{6,4},{8,10},{10,8},{12,14},{14,12},{16,18},{18,... | collective-permute-start | bytes 1769480 | tf_op jit(solution)/shard_map/ppermute | solution.py:68
  89.6 29.6 %collective-permute-start.13 = (bf16[8,48,1024]{2,1,0:T(8,128)(2,1)S(1)}, bf16[8,48,1024]{2,1,0:T(8,128)(2,1)S(1)}, u32[]{:S(2)}, u32[]{:S(2)}) collective-permute-start(bf16[8,48,1024]{2,1,0:T(8,128)(2,1)S(1)} %pad_maximum_fusion.2.refs_0_), channel_id=1, source_target_pairs={{0,4},{2,6},{4,0},{6,2},{8,12},{10,14},{12,8},{14,10},{16,20},{18,... | collective-permute-start | bytes 2359304 | tf_op jit(solution)/shard_map/ppermute | solution.py:68
  92.3 31.0 %copy-start.41 = (s32[1,2]{1,0:T(1,128)S(1)}, s32[1,2]{1,0:T(1,128)}, u32[]{:S(2)}) copy-start(s32[1,2]{1,0:T(1,128)} %param.21) | copy-start | bytes 28
  92.4 323.7 %reduce-scatter.5.cloned.1.call-start = ((), (), s32[]{:S(2)}) async-start(), calls=%async_computation.3 | async-start | bytes 2359296 | tf_op jit(solution)/shard_map/reduce_scatter | solution.py:408
  92.9 14.5 %collective-permute-start.26 = (bf16[8,48,768]{2,1,0:T(8,128)(2,1)S(1)}, bf16[8,48,768]{2,1,0:T(8,128)(2,1)S(1)}, u32[]{:S(2)}, u32[]{:S(2)}) collective-permute-start(bf16[8,48,768]{2,1,0:T(8,128)(2,1)S(1)} %pad_maximum_fusion.6.refs_0_), channel_id=1, source_target_pairs={{0,1},{1,0},{2,3},{3,2},{4,5},{5,4},{6,7},{7,6},{8,9},{9,8},{10,11... | collective-permute-start | bytes 1769480 | tf_op jit(solution)/shard_map/ppermute | solution.py:72
  98.3 24.4 %collective-permute-start.15 = (bf16[8,48,896]{2,1,0:T(8,128)(2,1)S(1)}, bf16[8,48,896]{2,1,0:T(8,128)(2,1)}, u32[]{:S(2)}, u32[]{:S(2)}) collective-permute-start(bf16[8,48,896]{2,1,0:T(8,128)(2,1)S(1)} %pad_maximum_fusion.4.refs_2_), channel_id=1, source_target_pairs={{0,2},{2,0},{4,6},{6,4},{8,10},{10,8},{12,14},{14,12},{16,18},{18,... | collective-permute-start | bytes 2064392 | tf_op jit(solution)/shard_map/ppermute | solution.py:68
  102.5 19.4 %collective-permute-start.28 = (bf16[8,48,768]{2,1,0:T(8,128)(2,1)S(1)}, bf16[8,48,768]{2,1,0:T(8,128)(2,1)S(1)}, u32[]{:S(2)}, u32[]{:S(2)}) collective-permute-start(bf16[8,48,768]{2,1,0:T(8,128)(2,1)S(1)} %pad_maximum_fusion.7.refs_2_), channel_id=1, source_target_pairs={{0,1},{1,0},{2,3},{3,2},{4,5},{5,4},{6,7},{7,6},{8,9},{9,8},{10,11... | collective-permute-start | bytes 1769480 | tf_op jit(solution)/shard_map/ppermute | solution.py:72
  107.3 15.9 %collective-permute-start.27 = (bf16[8,48,768]{2,1,0:T(8,128)(2,1)}, bf16[8,48,768]{2,1,0:T(8,128)(2,1)}, u32[]{:S(2)}, u32[]{:S(2)}) collective-permute-start(bf16[8,48,768]{2,1,0:T(8,128)(2,1)} %collective-permute-done.23.refs_1_), channel_id=1, source_target_pairs={{0,1},{1,0},{2,3},{3,2},{4,5},{5,4},{6,7},{7,6},{8,9},{9,8},{10,11... | collective-permute-start | bytes 1769480 | tf_op jit(solution)/shard_map/ppermute | solution.py:72
  108.2 30.8 %collective-permute-start.16 = (bf16[8,48,1024]{2,1,0:T(8,128)(2,1)S(1)}, bf16[8,48,1024]{2,1,0:T(8,128)(2,1)}, u32[]{:S(2)}, u32[]{:S(2)}) collective-permute-start(bf16[8,48,1024]{2,1,0:T(8,128)(2,1)S(1)} %pad_maximum_fusion.2.refs_0_), channel_id=1, source_target_pairs={{0,1},{1,0},{2,3},{3,2},{4,5},{5,4},{6,7},{7,6},{8,9},{9,8},{10,11... | collective-permute-start | bytes 2359304 | tf_op jit(solution)/shard_map/ppermute | solution.py:72
  119.2 19.8 %collective-permute-start.17 = (bf16[8,48,1024]{2,1,0:T(8,128)(2,1)S(1)}, bf16[8,48,1024]{2,1,0:T(8,128)(2,1)}, u32[]{:S(2)}, u32[]{:S(2)}) collective-permute-start(bf16[8,48,1024]{2,1,0:T(8,128)(2,1)S(1)} %collective-permute-done.13.refs_1_), channel_id=1, source_target_pairs={{0,1},{1,0},{2,3},{3,2},{4,5},{5,4},{6,7},{7,6},{8,9},{9,8},{10,11... | collective-permute-start | bytes 2359304 | tf_op jit(solution)/shard_map/ppermute | solution.py:72
  122.7 16.3 %collective-permute-start.18 = (bf16[8,48,896]{2,1,0:T(8,128)(2,1)S(1)}, bf16[8,48,896]{2,1,0:T(8,128)(2,1)}, u32[]{:S(2)}, u32[]{:S(2)}) collective-permute-start(bf16[8,48,896]{2,1,0:T(8,128)(2,1)S(1)} %pad_maximum_fusion.4.refs_2_), channel_id=1, source_target_pairs={{0,1},{1,0},{2,3},{3,2},{4,5},{5,4},{6,7},{7,6},{8,9},{9,8},{10,11... | collective-permute-start | bytes 2064392 | tf_op jit(solution)/shard_map/ppermute | solution.py:72
  122.7 16.3 %collective-permute-start.19 = (bf16[8,48,896]{2,1,0:T(8,128)(2,1)}, bf16[8,48,896]{2,1,0:T(8,128)(2,1)}, u32[]{:S(2)}, u32[]{:S(2)}) collective-permute-start(bf16[8,48,896]{2,1,0:T(8,128)(2,1)} %collective-permute-done.15.refs_3_), channel_id=1, source_target_pairs={{0,1},{1,0},{2,3},{3,2},{4,5},{5,4},{6,7},{7,6},{8,9},{9,8},{10,11... | collective-permute-start | bytes 2064392 | tf_op jit(solution)/shard_map/ppermute | solution.py:72
  123.2 9.6 %collective-permute-start.29 = (bf16[8,48,768]{2,1,0:T(8,128)(2,1)}, bf16[8,48,768]{2,1,0:T(8,128)(2,1)}, u32[]{:S(2)}, u32[]{:S(2)}) collective-permute-start(bf16[8,48,768]{2,1,0:T(8,128)(2,1)} %collective-permute-done.25.refs_3_), channel_id=1, source_target_pairs={{0,1},{1,0},{2,3},{3,2},{4,5},{5,4},{6,7},{7,6},{8,9},{9,8},{10,11... | collective-permute-start | bytes 1769480 | tf_op jit(solution)/shard_map/ppermute | solution.py:72
  153.0 44.0 %copy-start.12 = (bf16[1,1,512,768]{3,2,1,0:T(8,128)(2,1)S(1)}, bf16[1,1,512,768]{3,2,1,0:T(8,128)(2,1)}, u32[]{:S(2)}) copy-start(bf16[1,1,512,768]{3,2,1,0:T(8,128)(2,1)} %param.20) | copy-start | bytes 2359300
  153.0 44.0 %copy-start.40 = (f32[768]{0:T(1024)S(1)}, f32[768]{0:T(1024)}, u32[]{:S(2)}) copy-start(f32[768]{0:T(1024)} %get-tuple-element.249) | copy-start | bytes 9220
  199.5 141.7 %copy-start.17 = (f32[512,768]{1,0:T(8,128)}, f32[512,768]{1,0:T(8,128)S(1)}, u32[]{:S(2)}) copy-start(f32[512,768]{1,0:T(8,128)S(1)} %get-tuple-element.321) | copy-start | bytes 4718596
  324.8 91.3 %reduce-scatter.3.cloned.1.call-start = ((), (), s32[]{:S(2)}) async-start(), calls=%async_computation.2 | async-start | bytes 2359296 | tf_op jit(solution)/shard_map/reduce_scatter | solution.py:405
  340.0 27.3 %collective-permute-start.51 = (bf16[16,48,768]{2,1,0:T(8,128)(2,1)}, bf16[16,48,768]{2,1,0:T(8,128)(2,1)}, u32[]{:S(2)}, u32[]{:S(2)}) collective-permute-start(bf16[16,48,768]{2,1,0:T(8,128)(2,1)} %get-tuple-element.135), channel_id=1, source_target_pairs={{0,1},{1,0},{2,3},{3,2},{4,5},{5,4},{6,7},{7,6},{8,9},{9,8},{10,11... | collective-permute-start | bytes 3538952 | tf_op jit(solution)/shard_map/ppermute | solution.py:72
  357.0 16.2 %collective-permute-start.42 = (bf16[16,48,896]{2,1,0:T(8,128)(2,1)}, bf16[16,48,896]{2,1,0:T(8,128)(2,1)}, u32[]{:S(2)}, u32[]{:S(2)}) collective-permute-start(bf16[16,48,896]{2,1,0:T(8,128)(2,1)} %get-tuple-element.131), channel_id=1, source_target_pairs={{0,1},{1,0},{2,3},{3,2},{4,5},{5,4},{6,7},{7,6},{8,9},{9,8},{10,11... | collective-permute-start | bytes 4128776 | tf_op jit(solution)/shard_map/ppermute | solution.py:72
  357.4 30.0 %collective-permute-start.39 = (bf16[16,48,1024]{2,1,0:T(8,128)(2,1)}, bf16[16,48,1024]{2,1,0:T(8,128)(2,1)}, u32[]{:S(2)}, u32[]{:S(2)}) collective-permute-start(bf16[16,48,1024]{2,1,0:T(8,128)(2,1)} %get-tuple-element.129), channel_id=1, source_target_pairs={{0,1},{1,0},{2,3},{3,2},{4,5},{5,4},{6,7},{7,6},{8,9},{9,8},{10,11... | collective-permute-start | bytes 4718600 | tf_op jit(solution)/shard_map/ppermute | solution.py:72
  357.5 12.8 %collective-permute-start.48 = (bf16[16,48,768]{2,1,0:T(8,128)(2,1)}, bf16[16,48,768]{2,1,0:T(8,128)(2,1)}, u32[]{:S(2)}, u32[]{:S(2)}) collective-permute-start(bf16[16,48,768]{2,1,0:T(8,128)(2,1)} %get-tuple-element.133), channel_id=1, source_target_pairs={{0,1},{1,0},{2,3},{3,2},{4,5},{5,4},{6,7},{7,6},{8,9},{9,8},{10,11... | collective-permute-start | bytes 3538952 | tf_op jit(solution)/shard_map/ppermute | solution.py:72
  369.4 15.0 %collective-permute-start.52 = (bf16[8,48,768]{2,1,0:T(8,128)(2,1)S(1)}, bf16[8,48,768]{2,1,0:T(8,128)(2,1)S(1)}, u32[]{:S(2)}, u32[]{:S(2)}) collective-permute-start(bf16[8,48,768]{2,1,0:T(8,128)(2,1)S(1)} %slice.345), channel_id=1, source_target_pairs={{0,2},{2,0},{4,6},{6,4},{8,10},{10,8},{12,14},{14,12},{16,18},{18,... | collective-permute-start | bytes 1769480 | tf_op jit(solution)/shard_map/ppermute | solution.py:68
  371.9 14.5 %collective-permute-start.49 = (bf16[8,48,768]{2,1,0:T(8,128)(2,1)S(1)}, bf16[8,48,768]{2,1,0:T(8,128)(2,1)S(1)}, u32[]{:S(2)}, u32[]{:S(2)}) collective-permute-start(bf16[8,48,768]{2,1,0:T(8,128)(2,1)S(1)} %slice.341), channel_id=1, source_target_pairs={{0,4},{2,6},{4,0},{6,2},{8,12},{10,14},{12,8},{14,10},{16,20},{18,... | collective-permute-start | bytes 1769480 | tf_op jit(solution)/shard_map/ppermute | solution.py:68
  375.0 31.2 %collective-permute-start.43 = (bf16[8,48,896]{2,1,0:T(8,128)(2,1)S(1)}, bf16[8,48,896]{2,1,0:T(8,128)(2,1)S(1)}, u32[]{:S(2)}, u32[]{:S(2)}) collective-permute-start(bf16[8,48,896]{2,1,0:T(8,128)(2,1)S(1)} %slice.328), channel_id=1, source_target_pairs={{0,2},{2,0},{4,6},{6,4},{8,10},{10,8},{12,14},{14,12},{16,18},{18,... | collective-permute-start | bytes 2064392 | tf_op jit(solution)/shard_map/ppermute | solution.py:68
  384.5 7.3 %collective-permute-start.53 = (bf16[4,48,768]{2,1,0:T(8,128)(2,1)S(1)}, bf16[4,48,768]{2,1,0:T(8,128)(2,1)S(1)}, u32[]{:S(2)}, u32[]{:S(2)}) collective-permute-start(bf16[4,48,768]{2,1,0:T(8,128)(2,1)S(1)} %slice.347), channel_id=1, source_target_pairs={{0,4},{2,6},{4,0},{6,2},{8,12},{10,14},{12,8},{14,10},{16,20},{18,... | collective-permute-start | bytes 884744 | tf_op jit(solution)/shard_map/ppermute | solution.py:68
  386.6 18.8 %collective-permute-start.50 = (bf16[4,48,768]{2,1,0:T(8,128)(2,1)S(1)}, bf16[4,48,768]{2,1,0:T(8,128)(2,1)S(1)}, u32[]{:S(2)}, u32[]{:S(2)}) collective-permute-start(bf16[4,48,768]{2,1,0:T(8,128)(2,1)S(1)} %slice.343), channel_id=1, source_target_pairs={{0,2},{2,0},{4,6},{6,4},{8,10},{10,8},{12,14},{14,12},{16,18},{18,... | collective-permute-start | bytes 884744 | tf_op jit(solution)/shard_map/ppermute | solution.py:68
  389.5 19.7 %collective-permute-start.40 = (bf16[8,48,1024]{2,1,0:T(8,128)(2,1)S(1)}, bf16[8,48,1024]{2,1,0:T(8,128)(2,1)S(1)}, u32[]{:S(2)}, u32[]{:S(2)}) collective-permute-start(bf16[8,48,1024]{2,1,0:T(8,128)(2,1)S(1)} %slice.324), channel_id=1, source_target_pairs={{0,4},{2,6},{4,0},{6,2},{8,12},{10,14},{12,8},{14,10},{16,20},{18,... | collective-permute-start | bytes 2359304 | tf_op jit(solution)/shard_map/ppermute | solution.py:68
  405.5 7.8 %collective-permute-start.54 = (bf16[2,48,1536]{2,1,0:T(8,128)(2,1)S(1)}, bf16[2,48,1536]{2,1,0:T(8,128)(2,1)S(1)}, u32[]{:S(2)}, u32[]{:S(2)}) collective-permute-start(bf16[2,48,1536]{2,1,0:T(8,128)(2,1)S(1)} %pad_maximum_fusion.14), channel_id=1, source_target_pairs={{0,8},{2,10},{4,12},{6,14},{8,0},{10,2},{12,4},{14,6},{16,24},{18,... | collective-permute-start | bytes 884744 | tf_op jit(solution)/shard_map/ppermute | solution.py:68
  406.4 28.7 %collective-permute-start.44 = (bf16[4,48,896]{2,1,0:T(8,128)(2,1)S(1)}, bf16[4,48,896]{2,1,0:T(8,128)(2,1)}, u32[]{:S(2)}, u32[]{:S(2)}) collective-permute-start(bf16[4,48,896]{2,1,0:T(8,128)(2,1)S(1)} %slice.330), channel_id=1, source_target_pairs={{0,4},{2,6},{4,0},{6,2},{8,12},{10,14},{12,8},{14,10},{16,20},{18,... | collective-permute-start | bytes 1032200 | tf_op jit(solution)/shard_map/ppermute | solution.py:68
  411.2 30.3 %collective-permute-start.41 = (bf16[4,48,1024]{2,1,0:T(8,128)(2,1)}, bf16[4,48,1024]{2,1,0:T(8,128)(2,1)}, u32[]{:S(2)}, u32[]{:S(2)}) collective-permute-start(bf16[4,48,1024]{2,1,0:T(8,128)(2,1)} %slice.326), channel_id=1, source_target_pairs={{0,2},{2,0},{4,6},{6,4},{8,10},{10,8},{12,14},{14,12},{16,18},{18,... | collective-permute-start | bytes 1179656 | tf_op jit(solution)/shard_map/ppermute | solution.py:68
  414.1 22.2 %collective-permute-start.55 = (bf16[1,48,1536]{2,1,0:T(8,128)(2,1)S(1)}, bf16[1,48,1536]{2,1,0:T(8,128)(2,1)}, u32[]{:S(2)}, u32[]{:S(2)}) collective-permute-start(bf16[1,48,1536]{2,1,0:T(8,128)(2,1)S(1)} %slice.351), channel_id=1, source_target_pairs={{0,16},{2,18},{4,20},{6,22},{8,24},{10,26},{12,28},{14,30},{16,0},... | collective-permute-start | bytes 442376 | tf_op jit(solution)/shard_map/ppermute | solution.py:68
  432.7 10.2 %collective-permute-start.33 = (bf16[16,48,640]{2,1,0:T(8,128)(2,1)}, bf16[16,48,640]{2,1,0:T(8,128)(2,1)}, u32[]{:S(2)}, u32[]{:S(2)}) collective-permute-start(bf16[16,48,640]{2,1,0:T(8,128)(2,1)} %get-tuple-element.127), channel_id=1, source_target_pairs={{0,1},{1,0},{2,3},{3,2},{4,5},{5,4},{6,7},{7,6},{8,9},{9,8},{10,11... | collective-permute-start | bytes 2949128 | tf_op jit(solution)/shard_map/ppermute | solution.py:72
  436.2 9.4 %collective-permute-start.30 = (bf16[16,48,640]{2,1,0:T(8,128)(2,1)S(1)}, bf16[16,48,640]{2,1,0:T(8,128)(2,1)}, u32[]{:S(2)}, u32[]{:S(2)}) collective-permute-start(bf16[16,48,640]{2,1,0:T(8,128)(2,1)S(1)} %get-tuple-element.125), channel_id=1, source_target_pairs={{0,1},{1,0},{2,3},{3,2},{4,5},{5,4},{6,7},{7,6},{8,9},{9,8},{10,11... | collective-permute-start | bytes 2949128 | tf_op jit(solution)/shard_map/ppermute | solution.py:72
  442.8 9.7 %collective-permute-start.45 = (bf16[2,48,1920]{2,1,0:T(8,128)(2,1)S(1)}, bf16[2,48,1920]{2,1,0:T(8,128)(2,1)S(1)}, u32[]{:S(2)}, u32[]{:S(2)}) collective-permute-start(bf16[2,48,1920]{2,1,0:T(8,128)(2,1)S(1)} %pad_maximum_fusion.11), channel_id=1, source_target_pairs={{0,8},{2,10},{4,12},{6,14},{8,0},{10,2},{12,4},{14,6},{16,24},{18,... | collective-permute-start | bytes 1105928 | tf_op jit(solution)/shard_map/ppermute | solution.py:68
  444.4 12.1 %collective-permute-start.34 = (bf16[8,48,640]{2,1,0:T(8,128)(2,1)S(1)}, bf16[8,48,640]{2,1,0:T(8,128)(2,1)S(1)}, u32[]{:S(2)}, u32[]{:S(2)}) collective-permute-start(bf16[8,48,640]{2,1,0:T(8,128)(2,1)S(1)} %slice.311), channel_id=1, source_target_pairs={{0,2},{2,0},{4,6},{6,4},{8,10},{10,8},{12,14},{14,12},{16,18},{18,... | collective-permute-start | bytes 1474568 | tf_op jit(solution)/shard_map/ppermute | solution.py:68
  447.1 11.7 %collective-permute-start.31 = (bf16[8,48,640]{2,1,0:T(8,128)(2,1)S(1)}, bf16[8,48,640]{2,1,0:T(8,128)(2,1)S(1)}, u32[]{:S(2)}, u32[]{:S(2)}) collective-permute-start(bf16[8,48,640]{2,1,0:T(8,128)(2,1)S(1)} %slice.307), channel_id=1, source_target_pairs={{0,4},{2,6},{4,0},{6,2},{8,12},{10,14},{12,8},{14,10},{16,20},{18,... | collective-permute-start | bytes 1474568 | tf_op jit(solution)/shard_map/ppermute | solution.py:68
  452.7 13.3 %collective-permute-start.46 = (bf16[1,48,1920]{2,1,0:T(8,128)(2,1)S(1)}, bf16[1,48,1920]{2,1,0:T(8,128)(2,1)S(1)}, u32[]{:S(2)}, u32[]{:S(2)}) collective-permute-start(bf16[1,48,1920]{2,1,0:T(8,128)(2,1)S(1)} %slice.334), channel_id=1, source_target_pairs={{0,16},{2,18},{4,20},{6,22},{8,24},{10,26},{12,28},{14,30},{16,0},... | collective-permute-start | bytes 552968 | tf_op jit(solution)/shard_map/ppermute | solution.py:68
  456.7 7.9 %collective-permute-start.35 = (bf16[4,48,640]{2,1,0:T(8,128)(2,1)S(1)}, bf16[4,48,640]{2,1,0:T(8,128)(2,1)S(1)}, u32[]{:S(2)}, u32[]{:S(2)}) collective-permute-start(bf16[4,48,640]{2,1,0:T(8,128)(2,1)S(1)} %slice.313), channel_id=1, source_target_pairs={{0,4},{2,6},{4,0},{6,2},{8,12},{10,14},{12,8},{14,10},{16,20},{18,... | collective-permute-start | bytes 737288 | tf_op jit(solution)/shard_map/ppermute | solution.py:68
  459.0 5.6 %collective-permute-start.32 = (bf16[4,48,640]{2,1,0:T(8,128)(2,1)S(1)}, bf16[4,48,640]{2,1,0:T(8,128)(2,1)S(1)}, u32[]{:S(2)}, u32[]{:S(2)}) collective-permute-start(bf16[4,48,640]{2,1,0:T(8,128)(2,1)S(1)} %slice.309), channel_id=1, source_target_pairs={{0,2},{2,0},{4,6},{6,4},{8,10},{10,8},{12,14},{14,12},{16,18},{18,... | collective-permute-start | bytes 737288 | tf_op jit(solution)/shard_map/ppermute | solution.py:68
  464.7 5.3 %collective-permute-start.36 = (bf16[2,48,1280]{2,1,0:T(8,128)(2,1)S(1)}, bf16[2,48,1280]{2,1,0:T(8,128)(2,1)S(1)}, u32[]{:S(2)}, u32[]{:S(2)}) collective-permute-start(bf16[2,48,1280]{2,1,0:T(8,128)(2,1)S(1)} %pad_maximum_fusion.17), channel_id=1, source_target_pairs={{0,8},{2,10},{4,12},{6,14},{8,0},{10,2},{12,4},{14,6},{16,24},{18,... | collective-permute-start | bytes 737288 | tf_op jit(solution)/shard_map/ppermute | solution.py:68
  466.1 5.0 %collective-permute-start.47 = (f32[24,1920]{1,0:T(8,128)S(1)}, f32[24,1920]{1,0:T(8,128)S(1)}, u32[]{:S(2)}, u32[]{:S(2)}) collective-permute-start(f32[24,1920]{1,0:T(8,128)S(1)} %dynamic-slice_bitcast_fusion), channel_id=1, source_target_pairs={{0,1},{1,0},{2,3},{3,2},{4,5},{5,4},{6,7},{7,6},{8,9},{9,8},{10,11... | collective-permute-start | bytes 552968 | tf_op jit(solution)/shard_map/ppermute | solution.py:72
  470.1 6.0 %collective-permute-start.37 = (bf16[1,48,1280]{2,1,0:T(8,128)(2,1)S(1)}, bf16[1,48,1280]{2,1,0:T(8,128)(2,1)S(1)}, u32[]{:S(2)}, u32[]{:S(2)}) collective-permute-start(bf16[1,48,1280]{2,1,0:T(8,128)(2,1)S(1)} %slice.317), channel_id=1, source_target_pairs={{0,16},{2,18},{4,20},{6,22},{8,24},{10,26},{12,28},{14,30},{16,0},... | collective-permute-start | bytes 368648 | tf_op jit(solution)/shard_map/ppermute | solution.py:68
  476.2 6.7 %collective-permute-start.38 = (f32[24,1280]{1,0:T(8,128)S(1)}, f32[24,1280]{1,0:T(8,128)S(1)}, u32[]{:S(2)}, u32[]{:S(2)}) collective-permute-start(f32[24,1280]{1,0:T(8,128)S(1)} %dynamic-slice_bitcast_fusion.1), channel_id=1, source_target_pairs={{0,1},{1,0},{2,3},{3,2},{4,5},{5,4},{6,7},{7,6},{8,9},{9,8},{10,11... | collective-permute-start | bytes 368648 | tf_op jit(solution)/shard_map/ppermute | solution.py:72
  (47 other events, 261.2 us)
Sparse Core Ops, SparseCore 0:
  68.2 9.4 all-gather.4
  92.5 12.0 all-gather.6
  324.9 8.9 reduce-scatter.4
  367.4 8.8 reduce-scatter.2

commit v2 on v0

v2 whole, which is shorter than its diff:
```python
import functools

import jax
import jax.numpy as jnp
from jax import lax
from jax.experimental import pallas as pl
from jax.experimental.pallas import tpu as pltpu
from jax.sharding import PartitionSpec as P

HEAD_DIM = 64
LANES = 128
EPSILON = 1e-05
NEG_FILL = -1e30
VMEM_BYTES = 56 * 1024 * 1024
LOW = jnp.bfloat16
FULL = jnp.float32
SMALL = 8
GELU_IN = 0.7978845608028654
GELU_CUBE = 0.044715


def dot_nt(left, right):
    return lax.dot_general(left, right, (((1,), (1,)), ((), ())), preferred_element_type=jnp.float32)


def dot_nn(left, right):
    return lax.dot_general(left, right, (((1,), (0,)), ((), ())), preferred_element_type=jnp.float32)


def dot_tn(left, right):
    return lax.dot_general(left, right, (((0,), (0,)), ((), ())), preferred_element_type=jnp.float32)


def swap_chip(value, count, mask):
    return lax.ppermute(value, "fsdp", [(i, i ^ mask) for i in range(count)])


def swap_core(value, count):
    return lax.ppermute(value, "ctx", [(i, i ^ 1) for i in range(count)])


def after(values, others):
    return lax.optimization_barrier((values, others))[0]


class Layout:
    def __init__(self, fsdp, n_ctx, rows):
        self.fsdp, self.n_ctx = fsdp, n_ctx
        self.merge = 0
        while (rows << self.merge) % 16:
            self.merge += 1
        self.rows = rows << self.merge
        self.chips = fsdp >> self.merge
        self.depth = self.chips // 4
        self.shares = n_ctx << self.merge

    def swap(self, value, offset):
        return swap_chip(value, self.fsdp, offset << self.merge)

    def merged(self, shard):
        for bit in range(self.merge):
            other = swap_chip(shard, self.fsdp, 1 << bit)
            first = ((lax.axis_index("fsdp") >> bit) & 1) == 0
            shard = jnp.concatenate([jnp.where(first, shard, other), jnp.where(first, other, shard)], axis=0)
        return shard


def gather_far(shard, lay, core):
    half = shard.shape[-1] // 2
    own = lax.dynamic_slice_in_dim(shard, core * half, half, 1)[None]
    return jnp.concatenate([own] + [lay.swap(own, 4 * j) for j in range(1, lay.depth)], axis=0)


def gather_near(held, lay):
    return held, lay.swap(held, 1), lay.swap(held, 2)


def gather_corner(near, lay):
    middle = lay.depth // 2
    return near + (lay.swap(near[2][:middle], 1), lay.swap(near[1][middle:], 2))


def gather_core(pieces, lay):
    return tuple(pieces) + tuple(swap_core(piece, lay.n_ctx) for piece in pieces)


def piece_offsets(lay):
    middle = lay.depth // 2
    whole = [[m ^ (4 * j) for j in range(lay.depth)] for m in range(4)]
    return [whole[0], whole[1], whole[2], whole[3][:middle], whole[3][middle:]]


def windows(lay, index_ref, half, blocks, model):
    chip, core = index_ref[0], index_ref[1]
    for other in (0, 1):
        side = (1 - core) if other else core
        for number, offsets in enumerate(piece_offsets(lay)):
            for place, offset in enumerate(offsets):
                origin = chip ^ offset
                if blocks == 1:
                    row = pl.multiple_of(origin * lay.rows, 16)
                    yield 5 * other + number, place, slice(None), pl.ds(row, lay.rows), pl.ds(pl.multiple_of(side * half, LANES), half)
                else:
                    for part in range(blocks // 2):
                        row = pl.multiple_of((origin * blocks + side * (blocks // 2) + part) * lay.rows, 16)
                        columns = slice(part * model, (part + 1) * model)
                        yield 5 * other + number, place, columns, pl.ds(row, lay.rows), slice(None)


def fill(whole, pieces, lay, index_ref, blocks=1):
    half = pieces[0].shape[2]
    for number, place, columns, row, column in windows(lay, index_ref, half, blocks, whole.shape[1]):
        whole[row, column] = pieces[number][place, :, columns]


def cut(whole, pieces, lay, index_ref, blocks=1):
    half = pieces[0].shape[2]
    for number, place, columns, row, column in windows(lay, index_ref, half, blocks, whole.shape[1]):
        pieces[number][place, :, columns] = whole[row, column]


def piece_shapes(lay, half):
    return [jax.ShapeDtypeStruct((len(offsets), lay.rows, half), LOW) for offsets in piece_offsets(lay)] * 2


def low_sum(*members):
    return sum(member.astype(FULL) for member in members).astype(LOW)


def scatter_core(pieces, lay):
    return tuple(low_sum(keep, swap_core(send, lay.n_ctx)) for keep, send in zip(pieces[:5], pieces[5:]))


def scatter_corner(sums, lay):
    middle = lay.depth // 2
    own, one, two, corner_low, corner_high = sums
    to_two = lay.swap(corner_low, 1)
    to_one = lay.swap(corner_high, 2)
    one = jnp.concatenate([one[:middle], low_sum(one[middle:], to_one)], axis=0)
    two = jnp.concatenate([low_sum(two[:middle], to_two), two[middle:]], axis=0)
    return own, one, two


def scatter_near(sums, lay):
    own, one, two = sums
    got_one, got_two = lay.swap(one, 1), lay.swap(two, 2)
    return [low_sum(own[j], got_one[j], got_two[j]) for j in range(lay.depth)]


def scatter_far(parts, lay):
    total = sum([parts[0].astype(FULL)] + [lay.swap(parts[j], 4 * j).astype(FULL) for j in range(1, lay.depth)])
    if lay.n_ctx > 2:
        groups = [list(range(0, lay.n_ctx, 2)), list(range(1, lay.n_ctx, 2))]
        total = lax.psum(total, "ctx", axis_index_groups=groups)
    for bit in range(lay.merge):
        total = total + swap_chip(total, lay.fsdp, 1 << bit)
    return total


def share_rows(total, lay, share):
    rows = total.shape[0] // lay.shares
    mine = lax.dynamic_slice_in_dim(total, share * rows, rows, 0)
    theirs = swap_core(lax.dynamic_slice_in_dim(total, (share ^ 1) * rows, rows, 0), lay.n_ctx)
    first = (share & 1) == 0
    return jnp.concatenate([jnp.where(first, mine, theirs), jnp.where(first, theirs, mine)], axis=1)


def share_blocks(total, lay, share, blocks):
    rows = total.shape[0]
    parts = blocks // 2
    if lay.shares > 2:
        parts = blocks
        theirs = swap_core(total, lay.n_ctx)
        first = (share & 1) == 0
        total = jnp.concatenate([jnp.where(first, total, theirs), jnp.where(first, theirs, total)], axis=1)
    stacked = jnp.moveaxis(total.reshape(rows, parts, -1), 1, 0).reshape(parts * rows, -1)
    if lay.shares > 2:
        count = stacked.shape[0] // lay.shares
        stacked = lax.dynamic_slice_in_dim(stacked, share * count, count, 0)
    return stacked


def call(kernel, out_shape, scalars, arrays, scratch=(), flops=0):
    moved = sum(member.size * member.dtype.itemsize for member in list(arrays) + list(out_shape))
    return pl.pallas_call(
        kernel,
        out_shape=out_shape,
        in_specs=[pl.BlockSpec(memory_space=pltpu.SMEM)] + [pl.BlockSpec(memory_space=pltpu.VMEM)] * len(arrays),
        out_specs=[pl.BlockSpec(memory_space=pltpu.VMEM)] * len(out_shape),
        scratch_shapes=list(scratch),
        compiler_params=pltpu.CompilerParams(vmem_limit_bytes=VMEM_BYTES),
        cost_estimate=pl.CostEstimate(flops=flops, bytes_accessed=moved, transcendentals=0),
    )(scalars, *arrays)


def shaped(rows, columns, dtype=LOW):
    return jax.ShapeDtypeStruct((rows, columns), dtype)


def normalised(values):
    average = jnp.mean(values, axis=-1, keepdims=True)
    centred = values - average
    scale = lax.rsqrt(jnp.mean(centred * centred, axis=-1, keepdims=True) + EPSILON)
    return centred * scale, scale


def normalised_back(grads, hat, scale):
    return (grads - jnp.mean(grads, axis=-1, keepdims=True) - hat * jnp.mean(grads * hat, axis=-1, keepdims=True)) * scale


def column_sum(values):
    return jnp.sum(values.astype(FULL), axis=0, keepdims=True)


def first_kernel(lay, index_ref, tokens, *refs):
    pieces, (normed_ref, query_ref, key_ref, value_ref, whole, small_ref) = refs[:10], refs[10:]
    model = tokens.shape[1]
    fill(whole, pieces, lay, index_ref)
    small = whole[:, 3 * model : 3 * model + LANES].astype(FULL).T
    small_ref[...] = small[: small_ref.shape[0], :]
    hat, scale = normalised(tokens[...].astype(FULL))
    normed = (hat * small_ref[0:1, :] + small_ref[1:2, :]).astype(LOW)
    normed_ref[...] = normed
    query_ref[...] = (dot_nn(normed, whole[:, :model]) + small_ref[2:3, :]).astype(LOW)
    key_ref[...] = dot_nn(normed, whole[:, model : 2 * model]).astype(LOW)
    value_ref[...] = (dot_nn(normed, whole[:, 2 * model : 3 * model]) + small_ref[3:4, :]).astype(LOW)


def hidden_kernel(lay, index_ref, mixed, tokens, small, fc_bias, *refs):
    pieces, (whole, middle_ref, normed_ref, active_ref, slope_ref) = refs[:10], refs[10:]
    model = tokens.shape[1]
    hidden = active_ref.shape[1]
    fill(whole, pieces, lay, index_ref)
    middle = tokens[...].astype(FULL) + dot_nn(mixed[...], whole[:, hidden:]) + small[4:5, :]
    middle_ref[...] = middle
    hat, scale = normalised(middle)
    normed = (hat * small[5:6, :] + small[6:7, :]).astype(LOW)
    normed_ref[...] = normed
    for start in range(0, hidden, model):
        columns = slice(start, start + model)
        pre = dot_nn(normed, whole[:, columns]) + fc_bias[:, columns]
        square = pre * pre
        bent = jnp.tanh(GELU_IN * (pre + GELU_CUBE * square * pre))
        active_ref[:, columns] = (0.5 * pre * (1.0 + bent)).astype(LOW)
        slope = 0.5 * (1.0 + bent) + 0.5 * pre * (1.0 - bent * bent) * (GELU_IN * (1.0 + 3.0 * GELU_CUBE * square))
        slope_ref[:, columns] = slope.astype(LOW)


def proj_grad_kernel(lay, blocks, index_ref, active, cotangent, *refs):
    pieces, (sum_ref, whole) = refs[:10], refs[10:]
    model = cotangent.shape[1]
    sum_ref[...] = column_sum(cotangent[...])
    for start in range(0, active.shape[1], model):
        columns = slice(start, start + model)
        whole[columns, :] = dot_tn(active[:, columns], cotangent[...]).astype(LOW)
    cut(whole, pieces, lay, index_ref, blocks)


def middle_kernel(lay, blocks, index_ref, active, slope, cotangent, middle_ref, small, weights, *refs):
    pieces = refs[:10]
    out_ref, d_pre_ref, d_middle_ref, d_branch_ref, d_mixed_ref, sums_ref, hidden_sums_ref, proj = refs[10:]
    model = cotangent.shape[1]
    hidden = active.shape[1]
    fill(proj, pieces, lay, index_ref, blocks)
    d_normed = None
    for start in range(0, hidden, model):
        columns = slice(start, start + model)
        d_active = dot_nt(cotangent[...], proj[columns, :])
        d_pre = (d_active * slope[:, columns].astype(FULL)).astype(LOW)
        d_pre_ref[:, columns] = d_pre
        hidden_sums_ref[:, columns] = column_sum(d_pre)
        part = dot_nt(d_pre, weights[:, columns])
        d_normed = part if d_normed is None else d_normed + part
    hat, scale = normalised(middle_ref[...])
    sums_ref[0:1, :] = column_sum(d_normed * hat)
    sums_ref[1:2, :] = column_sum(d_normed)
    d_middle = cotangent[...].astype(FULL) + normalised_back(d_normed * small[5:6, :], hat, scale)
    d_middle_ref[...] = d_middle
    d_branch = d_middle.astype(LOW)
    d_branch_ref[...] = d_branch
    sums_ref[2:3, :] = column_sum(d_branch)
    d_mixed_ref[...] = dot_nt(d_branch, weights[:, hidden:]).astype(LOW)
    out_ref[...] = (middle_ref[...] + dot_nn(active[...], proj[...]) + small[7:8, :]).astype(LOW)


def hidden_grad_kernel(lay, index_ref, normed, d_pre, mixed, d_branch, *refs):
    pieces, whole = refs[:10], refs[10]
    model = normed.shape[1]
    hidden = d_pre.shape[1]
    for start in range(0, hidden, model):
        columns = slice(start, start + model)
        whole[:, columns] = dot_tn(normed[...], d_pre[:, columns]).astype(LOW)
    whole[:, hidden:] = dot_tn(mixed[...], d_branch[...]).astype(LOW)
    cut(whole, pieces, lay, index_ref)


def last_kernel(lay, count, index_ref, tokens, small, normed, weights, d_middle, others, *refs):
    backs = refs[: 5 * count]
    pieces = refs[5 * count : 5 * count + 10]
    grad_ref, d_qkv, whole, sums = refs[5 * count + 10 :]
    model = tokens.shape[1]
    at = 0
    for number in range(count):
        d_query, d_key, d_key_got, d_value, d_value_got = backs[5 * number : 5 * number + 5]
        width = d_query.shape[1]
        d_qkv[:, at : at + width] = d_query[...]
        d_qkv[:, model + at : model + at + width] = (d_key[...].astype(FULL) + d_key_got[...].astype(FULL)).astype(LOW)
        d_qkv[:, 2 * model + at : 2 * model + at + width] = (
            d_value[...].astype(FULL) + d_value_got[...].astype(FULL)
        ).astype(LOW)
        at += width
    d_normed = dot_nt(d_qkv[...], weights[:, : 3 * model])
    hat, scale = normalised(tokens[...].astype(FULL))
    grad_ref[...] = d_middle[...] + normalised_back(d_normed * small[0:1, :], hat, scale)
    sums[...] = jnp.zeros_like(sums)
    sums[0 : others.shape[0], :] = others[...]
    sums[0:1, :] = column_sum(d_normed * hat)
    sums[1:2, :] = column_sum(d_normed)
    sums[2:3, :] = column_sum(d_qkv[:, :model])
    sums[3:4, :] = column_sum(d_qkv[:, 2 * model :])
    for start in range(0, 3 * model, model):
        columns = slice(start, start + model)
        whole[:, columns] = dot_tn(normed[...], d_qkv[:, columns]).astype(LOW)
    whole[:, 3 * model : 3 * model + LANES] = sums[...].T.astype(LOW)
    whole[:, 3 * model + LANES :] = jnp.zeros((model, whole.shape[1] - 3 * model - LANES), LOW)
    cut(whole, pieces, lay, index_ref)


def head_lanes(head):
    lanes = lax.broadcasted_iota(jnp.int32, (1, 2 * HEAD_DIM), 1)
    return (lanes < HEAD_DIM) if head == 0 else (lanes >= HEAD_DIM)


def at_or_before(block):
    query_at = lax.broadcasted_iota(jnp.int32, (block, block), 0)
    key_at = lax.broadcasted_iota(jnp.int32, (block, block), 1)
    return query_at >= key_at


def softmax_parts(scores, values):
    top = functools.reduce(jnp.maximum, [jnp.max(s, axis=1, keepdims=True) for s in scores])
    weights = [jnp.exp(s - top) for s in scores]
    total = sum(jnp.sum(w, axis=1, keepdims=True) for w in weights)
    out = sum(dot_nn(w.astype(jnp.bfloat16), v) for w, v in zip(weights, values))
    return top, total, out


def merge_parts(left, right):
    top = jnp.maximum(left[0], right[0])
    left_scale, right_scale = jnp.exp(left[0] - top), jnp.exp(right[0] - top)
    return (
        top,
        left[1] * left_scale + right[1] * right_scale,
        left[2] * left_scale + right[2] * right_scale,
    )


def attend_kernel(n_ctx, early_ref, query_ref, own_key, own_value, far_key, far_value, out_ref, lse_ref):
    block = query_ref.shape[0] // 2
    causal = at_or_before(block)
    results = []
    for head in (0, 1):
        lanes = head_lanes(head)
        zero = jnp.zeros((), jnp.bfloat16)

        def rows_of(start):
            return jnp.where(lanes, query_ref[pl.ds(start, block), :] * HEAD_DIM**-0.5, zero)

        def keys_of(start, far=False):
            return (far_key if far else own_key)[pl.ds(start, block), :]

        def values_of(start, far=False):
            return (far_value if far else own_value)[pl.ds(start, block), :]

        query_low, query_high = rows_of(0), rows_of(block)
        low = softmax_parts([jnp.where(causal, dot_nt(query_low, keys_of(0)), NEG_FILL)], [values_of(0)])
        seen = [(0, False)] + [(2 * other * block, True) for other in range(n_ctx - 1)]
        high = softmax_parts(
            [jnp.where(causal, dot_nt(query_high, keys_of(block)), NEG_FILL)]
            + [dot_nt(query_high, keys_of(*at)) for at in seen],
            [values_of(block)] + [values_of(*at) for at in seen],
        )
        for other in range(n_ctx - 1):
            early = early_ref[other + 1]
            query_at = pl.multiple_of((1 - early) * block, block)
            key_at = pl.multiple_of((2 * other + 1 - early) * block, block)
            top, total, out = softmax_parts([dot_nt(rows_of(query_at), keys_of(key_at, True))], [values_of(key_at, True)])
            low = merge_parts(low, (jnp.where(early == 1, top, NEG_FILL), total, out))
            high = merge_parts(high, (jnp.where(early == 1, NEG_FILL, top), total, out))
        results.append((low, high))
    lanes = head_lanes(0)
    for half in (0, 1):
        (top_a, total_a, out_a), (top_b, total_b, out_b) = results[0][half], results[1][half]
        rows = pl.ds(half * block, block)
        out_ref[rows, :] = jnp.where(lanes, out_a / total_a, out_b / total_b).astype(out_ref.dtype)
        lse_ref[rows, :] = jnp.where(lanes, top_a + jnp.log(total_a), top_b + jnp.log(total_b))


def attend_back_kernel(
    n_ctx,
    early_ref,
    query_ref,
    own_key,
    own_value,
    far_key,
    far_value,
    dmix_ref,
    out_ref,
    lse_ref,
    dq_ref,
    dk_ref,
    dv_ref,
    far_dk_ref,
    far_dv_ref,
    dq_sum,
    dk_own,
    dv_own,
    dk_far,
    dv_far,
):
    block = query_ref.shape[0] // 2
    causal = at_or_before(block)
    zero = jnp.zeros((), jnp.bfloat16)
    for total in (dq_sum, dk_own, dv_own, dk_far, dv_far):
        total[...] = jnp.zeros_like(total)
    for head in (0, 1):
        lanes = head_lanes(head)

        def pair(query_at, key_at, mask=None, far=False):
            key_ref, value_ref, dk_sum, dv_sum = (
                (far_key, far_value, dk_far, dv_far) if far else (own_key, own_value, dk_own, dv_own)
            )
            query_rows, key_rows = pl.ds(query_at, block), pl.ds(key_at, block)
            query = jnp.where(lanes, query_ref[query_rows, :] * HEAD_DIM**-0.5, zero)
            dmix = jnp.where(lanes, dmix_ref[query_rows, :], zero)
            keys = key_ref[key_rows, :]
            product = dmix.astype(jnp.float32) * out_ref[query_rows, :].astype(jnp.float32)
            delta = jnp.sum(product, axis=1, keepdims=True)
            lse = lse_ref[query_rows, head * HEAD_DIM : head * HEAD_DIM + 1]
            chances = jnp.exp(dot_nt(query, keys) - lse)
            if mask is not None:
                chances = jnp.where(mask, chances, 0.0)
            d_scores = (chances * (dot_nt(dmix, value_ref[key_rows, :]) - delta)).astype(jnp.bfloat16)
            dq_sum[query_rows, :] += dot_nn(d_scores, jnp.where(lanes, keys, zero))
            dk_sum[key_rows, :] += dot_tn(d_scores, query)
            dv_sum[key_rows, :] += dot_tn(chances.astype(jnp.bfloat16), dmix)

        pair(0, 0, causal)
        pair(block, block, causal)
        pair(block, 0)
        for other in range(n_ctx - 1):
            pair(block, 2 * other * block, far=True)
            early = early_ref[other + 1]
            pair(
                pl.multiple_of((1 - early) * block, block),
                pl.multiple_of((2 * other + 1 - early) * block, block),
                far=True,
            )
    dq_ref[...] = (dq_sum[...] * HEAD_DIM**-0.5).astype(dq_ref.dtype)
    for target, total in ((dk_ref, dk_own), (dv_ref, dv_own), (far_dk_ref, dk_far), (far_dv_ref, dv_far)):
        target[...] = total[...].astype(target.dtype)


def pair_spec(rows, start=0):
    return pl.BlockSpec((rows, 2 * HEAD_DIM), lambda pair: (0, start + pair))


def pair_spec(rows, start=0):
    return pl.BlockSpec((rows, 2 * HEAD_DIM), lambda pair: (0, start + pair))


def attend(early, queries, context, n_ctx):
    length, width = queries.shape
    return pl.pallas_call(
        functools.partial(attend_kernel, n_ctx),
        grid=(width // (2 * HEAD_DIM),),
        out_shape=[shaped(length, width), shaped(length, width, FULL)],
        in_specs=[pl.BlockSpec(memory_space=pltpu.SMEM)] + [pair_spec(member.shape[0]) for member in (queries,) + context],
        out_specs=[pair_spec(length)] * 2,
        compiler_params=pltpu.CompilerParams(vmem_limit_bytes=VMEM_BYTES),
        cost_estimate=pl.CostEstimate(
            flops=8 * n_ctx * length * length * width, bytes_accessed=14 * length * width, transcendentals=length * length * n_ctx
        ),
    )(early, queries, *context)


def attend_back(early, queries, context, dmix, out, lse, n_ctx, start, stop):
    length = queries.shape[0]
    others = context[2].shape[0]
    span = (stop - start) * 2 * HEAD_DIM
    operands = (queries,) + context + (dmix, out, lse)
    heights = [length, length, length, others, others]
    return pl.pallas_call(
        functools.partial(attend_back_kernel, n_ctx),
        grid=(stop - start,),
        out_shape=[shaped(height, span) for height in heights],
        in_specs=[pl.BlockSpec(memory_space=pltpu.SMEM)] + [pair_spec(member.shape[0], start) for member in operands],
        out_specs=[pair_spec(height) for height in heights],
        scratch_shapes=[pltpu.VMEM((height, 2 * HEAD_DIM), FULL) for height in heights],
        compiler_params=pltpu.CompilerParams(vmem_limit_bytes=VMEM_BYTES),
        cost_estimate=pl.CostEstimate(
            flops=20 * n_ctx * length * length * span, bytes_accessed=20 * length * span, transcendentals=length * length * n_ctx
        ),
    )(early, *operands)


def gather_ctx(own, n_ctx, ctx_index):
    if n_ctx == 2:
        return swap_core(own, n_ctx)
    whole = lax.all_gather(own, "ctx", axis=0, tiled=True)
    return jnp.roll(whole, -ctx_index * own.shape[0], axis=0)[own.shape[0] :]


def scatter_ctx(own, far, n_ctx, ctx_index):
    if n_ctx == 2:
        return own, swap_core(far, n_ctx)
    whole = jnp.roll(jnp.concatenate([own, far], axis=0), ctx_index * own.shape[0], axis=0)
    return lax.psum_scatter(whole, "ctx", scatter_dimension=0, tiled=True), jnp.zeros_like(own)


def body(
    tokens,
    pair_order,
    gain_one,
    bias_one,
    w_qkv,
    bias_q,
    bias_v,
    w_out,
    bias_out,
    gain_two,
    bias_two,
    w_fc,
    bias_fc,
    w_proj,
    bias_proj,
    cotangent,
):
    model = tokens.shape[-1]
    length = tokens.shape[2]
    fsdp, n_ctx = lax.axis_size("fsdp"), lax.axis_size("ctx")
    ctx_index = lax.axis_index("ctx")
    core = ctx_index & 1
    chip = lax.axis_index("fsdp")
    lay = Layout(fsdp, n_ctx, gain_one.shape[0])
    share = (chip & ((1 << lay.merge) - 1)) * n_ctx + ctx_index
    where = jnp.stack([chip >> lay.merge, core]).astype(jnp.int32)
    rows, depth = lay.rows, lay.depth
    tokens_in = tokens.reshape(length, model)
    cotangent_in = cotangent.reshape(length, model)
    vectors = [gain_one, bias_one, bias_q, bias_v, bias_out, gain_two, bias_two, bias_proj]
    bias_rows = lay.merged(bias_fc).reshape(-1, rows)
    blocks = bias_rows.shape[0]
    small_count = SMALL + blocks
    small_rows = jnp.concatenate([lay.merged(jnp.stack(vectors, axis=1)), bias_rows.T], axis=1)
    small_rows = jnp.pad(small_rows, ((0, 0), (0, 2 * LANES - small_count)))
    hidden = w_fc.shape[1]
    group_one = jnp.concatenate([lay.merged(w_qkv), small_rows], axis=1)
    group_two = jnp.concatenate([lay.merged(w_fc), lay.merged(w_out)], axis=1)
    group_three = jnp.moveaxis(lay.merged(w_proj).reshape(blocks, rows, model), 0, 1).reshape(rows, blocks * model)
    half_one, half_two, half_three = [member.shape[1] // 2 for member in (group_one, group_two, group_three)]

    far_one = gather_far(group_one, lay, core)
    group_two, group_three = after((group_two, group_three), far_one)
    far_two = gather_far(group_two, lay, core)
    near_one = gather_near(far_one, lay)
    corner_one = gather_corner(near_one, lay)
    corner_one, far_two, group_three = lax.optimization_barrier((corner_one, far_two, group_three))
    near_two = gather_near(far_two, lay)
    far_three = gather_far(group_three, lay, core)
    normed_one, queries, keys, values, whole_one, small = call(
        functools.partial(first_kernel, lay),
        [shaped(length, model)] * 4 + [shaped(model, 2 * half_one), shaped(16, model, FULL)],
        where,
        (tokens_in,) + gather_core(corner_one, lay),
        flops=6 * length * model * model,
    )
    context = (keys, values, gather_ctx(keys, n_ctx, ctx_index), gather_ctx(values, n_ctx, ctx_index))
    context, near_two, far_three = lax.optimization_barrier((context, near_two, far_three))
    corner_two = gather_corner(near_two, lay)
    pairs = jnp.roll(pair_order[0], -ctx_index)
    early = (pairs < pairs[0]).astype(jnp.int32)
    mixed, lse = attend(early, queries, context, n_ctx)
    mixed, corner_two, far_three = lax.optimization_barrier((mixed, corner_two, far_three))
    near_three = gather_near(far_three, lay)
    fc_bias = jnp.moveaxis(small[SMALL:small_count].reshape(blocks, lay.chips, rows), 0, 1).reshape(1, hidden)
    whole_two, middle, normed_two, active, slope = call(
        functools.partial(hidden_kernel, lay),
        [
            shaped(model, 2 * half_two),
            shaped(length, model, FULL),
            shaped(length, model),
            shaped(length, hidden),
            shaped(length, hidden),
        ],
        where,
        (mixed, tokens_in, small, fc_bias) + gather_core(corner_two, lay),
        flops=2 * length * model * (model + hidden),
    )
    active, near_three = lax.optimization_barrier((active, near_three))
    corner_three = gather_corner(near_three, lay)
    *share_three, sum_cotangent = call(
        functools.partial(proj_grad_kernel, lay, blocks),
        piece_shapes(lay, half_three) + [shaped(1, model, FULL)],
        where,
        (active, cotangent_in),
        [pltpu.VMEM((hidden, model), LOW)],
        flops=2 * length * model * hidden,
    )
    share_three, corner_three = lax.optimization_barrier((share_three, corner_three))
    share_three = scatter_core(share_three, lay)
    out_rows, d_pre, d_middle, d_branch, d_mixed, sums, hidden_sums = call(
        functools.partial(middle_kernel, lay, blocks),
        [
            shaped(length, model),
            shaped(length, hidden),
            shaped(length, model, FULL),
            shaped(length, model),
            shaped(length, model),
            shaped(8, model, FULL),
            shaped(1, hidden, FULL),
        ],
        where,
        (active, slope, cotangent_in, middle, small, whole_two) + gather_core(corner_three, lay),
        [pltpu.VMEM((hidden, model), LOW)],
        flops=6 * length * model * hidden,
    )
    share_three = scatter_corner(share_three, lay)
    d_pre, share_three = lax.optimization_barrier((d_pre, share_three))
    share_three = scatter_near(share_three, lay)
    share_two = call(
        functools.partial(hidden_grad_kernel, lay),
        piece_shapes(lay, half_two),
        where,
        (normed_two, d_pre, mixed, d_branch),
        [pltpu.VMEM((model, 2 * half_two), LOW)],
        flops=2 * length * model * (model + hidden),
    )
    d_mixed, share_two, share_three = lax.optimization_barrier((d_mixed, share_two, share_three))
    share_two = scatter_core(share_two, lay)
    total_three = scatter_far(share_three, lay)
    share_two = scatter_corner(share_two, lay)
    pair_count = model // (2 * HEAD_DIM)
    cuts = [0, pair_count // 3, pair_count]
    backs = []
    for start, stop in zip(cuts[:-1], cuts[1:]):
        d_query, d_key, d_value, far_key, far_value = attend_back(
            early, queries, context, d_mixed, mixed, lse, n_ctx, start, stop
        )
        backs.append(
            (d_query,) + scatter_ctx(d_key, far_key, n_ctx, ctx_index) + scatter_ctx(d_value, far_value, n_ctx, ctx_index)
        )
        if start == 0:
            d_mixed, share_two, total_three, d_query = lax.optimization_barrier((d_mixed, share_two, total_three, d_query))
            share_two = scatter_near(share_two, lay)
    backs, share_two = lax.optimization_barrier((backs, share_two))
    total_two = scatter_far(share_two, lay)
    others = jnp.concatenate(
        [
            jnp.zeros((4, model), FULL),
            sums[2:3],
            sums[0:2],
            sum_cotangent,
            jnp.moveaxis(hidden_sums.reshape(lay.chips, lay.shares, blocks, rows // lay.shares), 2, 0).reshape(blocks, model),
            jnp.zeros((16 - small_count, model), FULL),
        ]
    )
    *share_one, grad_rows = call(
        functools.partial(last_kernel, lay, len(backs)),
        piece_shapes(lay, half_one) + [shaped(length, model, FULL)],
        where,
        (tokens_in, small, normed_one, whole_one, d_middle, others) + sum(backs, ()),
        [
            pltpu.VMEM((length, 3 * model), LOW),
            pltpu.VMEM((model, 2 * half_one), LOW),
            pltpu.VMEM((LANES, model), FULL),
        ],
        flops=12 * length * model * model,
    )
    share_one = scatter_core(share_one, lay)
    share_one = scatter_corner(share_one, lay)
    share_one = scatter_near(share_one, lay)
    share_one = share_rows(scatter_far(share_one, lay), lay, share)
    share_two = share_rows(total_two, lay, share)
    share_proj = share_blocks(total_three, lay, share, blocks)
    small_share = share_one[:, 3 * model : 3 * model + small_count].T
    names = ("gain_one", "bias_one", "bias_q", "bias_v", "bias_out", "gain_two", "bias_two", "bias_proj")
    small_grads = dict(zip(names, small_share))
    return (
        out_rows.reshape(tokens.shape),
        grad_rows.reshape(tokens.shape),
        small_grads["gain_one"],
        small_grads["bias_one"],
        share_one[:, : 3 * model],
        small_grads["bias_q"],
        small_grads["bias_v"],
        share_two[:, hidden:],
        small_grads["bias_out"],
        small_grads["gain_two"],
        small_grads["bias_two"],
        share_two[:, :hidden],
        small_share[SMALL:].reshape(-1),
        share_proj,
        small_grads["bias_proj"],
    )


def solution(mesh):
    placed = (
        P("fsdp", "ctx", None, None),
        P("fsdp", None),
        P("fsdp"),
        P("fsdp"),
        P("fsdp", None),
        P("fsdp"),
        P("fsdp"),
        P("fsdp", None),
        P("fsdp"),
        P("fsdp"),
        P("fsdp"),
        P("fsdp", None),
        P("fsdp"),
        P("fsdp", None),
        P("fsdp"),
        P("fsdp", "ctx", None, None),
    )
    return jax.shard_map(
        body,
        mesh=mesh,
        in_specs=placed,
        out_specs=(
            P("fsdp", "ctx", None, None),
            P("fsdp", "ctx", None, None),
            P(("fsdp", "ctx")),
            P(("fsdp", "ctx")),
            P(("fsdp", "ctx"), None),
            P(("fsdp", "ctx")),
            P(("fsdp", "ctx")),
            P(("fsdp", "ctx"), None),
            P(("fsdp", "ctx")),
            P(("fsdp", "ctx")),
            P(("fsdp", "ctx")),
            P(("fsdp", "ctx"), None),
            P(("fsdp", "ctx")),
            P(("fsdp", "ctx"), None),
            P(("fsdp", "ctx")),
        ),
        check_vma=False,
    )
```

time: 1020 us -> 291 us (0.29)
  waiting for transfers between devices: 631 us -> 73 us
  matrix products: 207 us -> 0 us
  blocking collectives: 106 us -> 0 us
  Pallas kernels: 0 us -> 105 us
  starting transfers between devices: 0.9 us -> 77.6 us
  local copies, waits for them, and re-layouts: 30.3 us -> 15.4 us
  between operations: 16.4 us -> 2.07 us
    reduce_scatter x6 -> x0, waiting for transfers between devices: 441 us -> none  [the longest x1 142 us: body(): lax.psum_scatter(grad_proj, ('fsdp', 'ctx'), scatter_dimension=0, tiled=T...]
    dot_general x96 -> x0, matrix products: 207 us -> none  [the longest x4 29.5 us: inner_rows(): lax.dot_general(left, right, (((0,), (0,)), ((), ())), preferred_element_...]
    all_gather x6 -> x0, waiting for transfers between devices: 187 us -> none  [the longest x1 80.2 us: body(): lax.all_gather(w_fc, 'fsdp', axis=0, tiled=True)]
    unnamed x2 -> x0, blocking collectives: 106 us -> none
    pallas_call x0 -> x9, Pallas kernels: none -> 105 us  [the longest x6 65.1 us: call(): pl.pallas_call(kernel, out_shape=out_shape, in_specs=[pl.BlockSpec(memory...]
    ppermute x0 -> x80, starting transfers between devices: none -> 77.6 us  [the longest x42 47.8 us: swap_chip(): return lax.ppermute(value, 'fsdp', [(i, i ^ mask) for i in range(count)])]
    ppermute x0 -> x80, waiting for transfers between devices: none -> 73 us  [the longest x42 62.7 us: swap_chip(): return lax.ppermute(value, 'fsdp', [(i, i ^ mask) for i in range(count)])]
    unnamed x62 -> x87, local copies, waits for them, and re-layouts: 23.9 us -> 1.35 us
  transfers between devices with their start and end apart: 12 -> 80, of which waited for: 11 -> 29; matrix products, arithmetic and copies ran while one was open for 13% -> 7% of each run, Pallas kernels for 0% -> 37%
where the time goes in v2:
time: 291 us; the launch traced here: 285 us
  Pallas kernels  105 us (36%)
  starting transfers between devices  77.6 us (27%)
  waiting for transfers between devices  73 us (25%)
  local copies, waits for them, and re-layouts  15.4 us (5%)
  other arithmetic  12.1 us (4%)
    pallas_call x6, Pallas kernels, call(): pl.pallas_call(kernel, out_shape=out_shape, in_specs=[pl.BlockSpec(memory...  65.1 us
    ppermute x42, waiting for transfers between devices, swap_chip(): return lax.ppermute(value, 'fsdp', [(i, i ^ mask) for i in range(count)])  62.7 us
    ppermute x42, starting transfers between devices, swap_chip(): return lax.ppermute(value, 'fsdp', [(i, i ^ mask) for i in range(count)])  47.8 us
    ppermute x38, starting transfers between devices, swap_core(): return lax.ppermute(value, 'ctx', [(i, i ^ 1) for i in range(count)])  29.8 us
    pallas_call x2, Pallas kernels, attend_back(): pl.pallas_call(functools.partial(attend_back_kernel, n_ctx), grid=(stop -...  26.4 us
    pallas_call x1, Pallas kernels, attend(): pl.pallas_call(functools.partial(attend_kernel, n_ctx), grid=(width // (2...  13.8 us
    ppermute x38, waiting for transfers between devices, swap_core(): return lax.ppermute(value, 'ctx', [(i, i ^ 1) for i in range(count)])  10.3 us
  transfers between devices with their start and end apart: 80, of which 29 were waited for; matrix products, arithmetic and copies ran while one was open for 7% of the time, Pallas kernels for 37%

profile of v2, /device:TPU:1, one launch (start us, length us, event | category | flops | bytes accessed | tf_op | source)
XLA Modules:
  0.0 285.4 jit_solution(3493999846846433460)
XLA Ops:
  3.4 2.2 collective-permute-start
  5.5 2.3 collective-permute-start.1
  8.6 1.7 collective-permute-done.1
  10.3 5.5 %collective-permute-done.2 = bf16[1,48,1280]{2,1,0:T(8,128)(2,1)S(1)} collective-permute-done((bf16[1,48,1280]{2,1,0:T(8,128)(2,1)S(1)}, bf16[1,48,1280]{2,1,0:T(8,128)(2,1)S(1)}, u32[]{:S(2)}, u32[]{:S(2)}) %collective-permute-start.2) | collective-permute-done | bytes 122912 | tf_op jit(solution)/shard_map/ppermute | solution.py:35
  15.8 1.3 collective-permute-start.4
  17.2 1.2 collective-permute-start.3
  19.4 2.6 collective-permute-start.7
  22.0 1.5 collective-permute-start.8
  23.5 1.1 collective-permute-start.9
  24.6 1.1 collective-permute-done.4.refs_2_
  25.7 1.0 slice.252
  26.6 1.3 collective-permute-start.5
  27.9 1.0 slice.253
  28.9 1.3 collective-permute-start.6
  30.2 4.5 %collective-permute-done.9 = bf16[1,48,1920]{2,1,0:T(8,128)(2,1)S(1)} collective-permute-done((bf16[1,48,1920]{2,1,0:T(8,128)(2,1)S(1)}, bf16[1,48,1920]{2,1,0:T(8,128)(2,1)S(1)}, u32[]{:S(2)}, u32[]{:S(2)}) %collective-permute-start.9) | collective-permute-done | bytes 184352 | tf_op jit(solution)/shard_map/ppermute | solution.py:35
  34.9 5.2 %collective-permute-start.10 = (bf16[4,48,1280]{2,1,0:T(8,128)(2,1)S(1)}, bf16[4,48,1280]{2,1,0:T(8,128)(2,1)}, u32[]{:S(2)}, u32[]{:S(2)}) collective-permute-start(bf16[4,48,1280]{2,1,0:T(8,128)(2,1)S(1)} %pad_maximum_fusion.6.refs_0_), channel_id=1, source_target_pairs={{0,1},{1,0},{2,3},{3,2},{4,5},{5,4},{6,7},{7,6},{8,9},{9,8},{10,11... | collective-permute-start | bytes 1474568 | tf_op jit(solution)/shard_map/ppermute | solution.py:39
  41.7 1.5 collective-permute-done.13.refs_8_
  44.1 7.2 %shard_map.271 = (bf16[512,768]{1,0:T(8,128)(2,1)}, bf16[512,768]{1,0:T(8,128)(2,1)}, bf16[512,768]{1,0:T(8,128)(2,1)}, bf16[512,768]{1,0:T(8,128)(2,1)}, bf16[768,2560]{1,0:T(8,128)(2,1)}, /*index=5*/f32[16,768]{1,0:T(8,128)}) custom-call(s32[2]{0:T(128)} %pad_add_fusion.index_ref, bf16[512,768]{1,0:T(8,128)(2,1)} %bitcast.84, ...), custom_call_target="tpu_custom_call" | custom-call | flops 1811939328 | bytes 11845632 | tf_op jit(solution)/shard_map/pallas_call | solution.py:185
  52.1 2.6 collective-permute-start.19
  54.8 3.8 %collective-permute-done.19 = bf16[1,48,1536]{2,1,0:T(8,128)(2,1)S(1)} collective-permute-done((bf16[1,48,1536]{2,1,0:T(8,128)(2,1)S(1)}, bf16[1,48,1536]{2,1,0:T(8,128)(2,1)S(1)}, u32[]{:S(2)}, u32[]{:S(2)}) %collective-permute-start.19) | collective-permute-done | bytes 147488 | tf_op jit(solution)/shard_map/ppermute | solution.py:35
  58.6 2.6 collective-permute-start.20
  61.2 6.8 %collective-permute-done.20 = bf16[1,48,1536]{2,1,0:T(8,128)(2,1)S(1)} collective-permute-done((bf16[1,48,1536]{2,1,0:T(8,128)(2,1)S(1)}, bf16[1,48,1536]{2,1,0:T(8,128)(2,1)S(1)}, u32[]{:S(2)}, u32[]{:S(2)}) %collective-permute-start.20) | collective-permute-done | bytes 147488 | tf_op jit(solution)/shard_map/ppermute | solution.py:35
  68.0 2.2 collective-permute-start.21
  70.3 3.6 %collective-permute-done.21 = bf16[1,48,1536]{2,1,0:T(8,128)(2,1)S(1)} collective-permute-done((bf16[1,48,1536]{2,1,0:T(8,128)(2,1)S(1)}, bf16[1,48,1536]{2,1,0:T(8,128)(2,1)S(1)}, u32[]{:S(2)}, u32[]{:S(2)}) %collective-permute-start.21) | collective-permute-done | bytes 147488 | tf_op jit(solution)/shard_map/ppermute | solution.py:35
  74.0 1.3 collective-permute-start.22
  76.6 13.8 %shard_map.272 = (bf16[512,768]{1,0:T(8,128)(2,1)}, f32[512,768]{1,0:T(8,128)}) custom-call(s32[2]{0:T(128)} %compare_convert_fusion.early_ref, bf16[512,768]{1,0:T(8,128)(2,1)} %get-tuple-element.165.query_ref, bf16[512,768]{1,0:T(8,128)(2,1)} %get-tuple-element.170.own_key, bf16[512,768]{1,0:T(8,128)(2,1)} %get-tuple-element.171.own_value, ...), custom_call_target="tpu_custom_call" | custom-call | flops 3221225472 | bytes 5505024 | tf_op jit(solution)/shard_map/pallas_call | solution.py:474
  90.4 2.9 %collective-permute-start.24 = (bf16[4,48,1920]{2,1,0:T(8,128)(2,1)S(1)}, bf16[4,48,1920]{2,1,0:T(8,128)(2,1)}, u32[]{:S(2)}, u32[]{:S(2)}) collective-permute-start(bf16[4,48,1920]{2,1,0:T(8,128)(2,1)S(1)} %pad_maximum_fusion.refs_0_), channel_id=1, source_target_pairs={{0,1},{1,0},{2,3},{3,2},{4,5},{5,4},{6,7},{7,6},{8,9},{9,8},{10,11... | collective-permute-start | bytes 2211848 | tf_op jit(solution)/shard_map/ppermute | solution.py:39
  94.4 1.9 collective-permute-done.27.refs_8_
  99.8 12.9 %shard_map.273 = (bf16[768,3840]{1,0:T(8,128)(2,1)}, f32[512,768]{1,0:T(8,128)}, bf16[512,768]{1,0:T(8,128)(2,1)}, bf16[512,3072]{1,0:T(8,128)(2,1)}, bf16[512,3072]{1,0:T(8,128)(2,1)}) custom-call(s32[2]{0:T(128)} %pad_add_fusion.index_ref, bf16[512,768]{1,0:T(8,128)(2,1)} %get-tuple-element.179.mixed.out_ref, bf16[512,768]{1,0:T(8,128)(2,1)} %bitcast.85, ...), custom_call_target="tpu_custom_call" | custom-call | flops 3019898880 | bytes 22081536 | tf_op jit(solution)/shard_map/pallas_call | solution.py:185
  112.7 1.0 slice.195
  114.2 1.0 slice.196
  116.0 7.0 %shard_map.274 = (bf16[4,48,1536]{2,1,0:T(8,128)(2,1)}, bf16[4,48,1536]{2,1,0:T(8,128)(2,1)}, bf16[4,48,1536]{2,1,0:T(8,128)(2,1)}, bf16[2,48,1536]{2,1,0:T(8,12...) custom-call(s32[2]{0:T(128)} %pad_add_fusion.index_ref, ...), custom_call_target="tpu_custom_call" | custom-call | flops 2415919104 | bytes 8653824 | tf_op jit(solution)/shard_map/pallas_call | solution.py:185
  123.0 1.7 collective-permute-start.43
  126.5 1.0 add_convert_fusion.14
  127.5 1.5 collective-permute-done.40
  129.4 1.0 add_convert_fusion.16
  132.7 1.0 collective-permute-start.44
  135.5 18.5 %shard_map.275 = (bf16[512,768]{1,0:T(8,128)(2,1)}, bf16[512,3072]{1,0:T(8,128)(2,1)}, f32[512,768]{1,0:T(8,128)}, bf16[512,768]{1,0:T(8,128)(2,1)}, bf16[512,76...) custom-call(s32[2]{0:T(128)} %pad_add_fusion.index_ref, bf16[512,3072]{1,0:T(8,128)(2,1)} %get-tuple-element.188.active, ...), custom_call_target="tpu_custom_call" | custom-call | flops 7247757312 | bytes 26431488 | tf_op jit(solution)/shard_map/pallas_call | solution.py:185
  155.8 8.4 %shard_map.276 = (bf16[4,48,1920]{2,1,0:T(8,128)(2,1)}, bf16[4,48,1920]{2,1,0:T(8,128)(2,1)}, bf16[4,48,1920]{2,1,0:T(8,128)(2,1)}, bf16[2,48,1920]{2,1,0:T(8,12...) custom-call(s32[2]{0:T(128)} %pad_add_fusion.index_ref, ...), custom_call_target="tpu_custom_call" | custom-call | flops 3019898880 | bytes 11403264 | tf_op jit(solution)/shard_map/pallas_call | solution.py:185
  164.2 4.3 %collective-permute-done.45 = bf16[4,48,1536]{2,1,0:T(8,128)(2,1)S(1)} collective-permute-done((bf16[4,48,1536]{2,1,0:T(8,128)(2,1)S(1)}, bf16[4,48,1536]{2,1,0:T(8,128)(2,1)S(1)}, u32[]{:S(2)}, u32[]{:S(2)}) %collective-permute-start.45) | collective-permute-done | bytes 589856 | tf_op jit(solution)/shard_map/ppermute | solution.py:35
  169.1 1.2 collective-permute-start.56
  170.3 1.7 collective-permute-start.57
  172.7 3.0 %collective-permute-start.54 = (bf16[2,48,1920]{2,1,0:T(8,128)(2,1)S(1)}, bf16[2,48,1920]{2,1,0:T(8,128)(2,1)S(1)}, u32[]{:S(2)}, u32[]{:S(2)}) collective-permute-start(bf16[2,48,1920]{2,1,0:T(8,128)(2,1)S(1)} %copy-done.30), channel_id=1, source_target_pairs={{0,1},{1,0},{2,3},{3,2},{4,5},{5,4},{6,7},{7,6},{8,9},{9,8},{10,11... | collective-permute-start | bytes 1105928 | tf_op jit(solution)/shard_map/ppermute | solution.py:39
  175.8 9.5 %shard_map.277 = (bf16[512,256]{1,0:T(8,128)(2,1)}, bf16[512,256]{1,0:T(8,128)(2,1)}, bf16[512,256]{1,0:T(8,128)(2,1)}, bf16[512,256]{1,0:T(8,128)(2,1)}, bf16[512,256]{1,0:T(8,128)(2,1)}) custom-call(s32[2]{0:T(128)} %compare_convert_fusion.early_ref, bf16[512,768]{1,0:T(8,128)(2,1)} %get-tuple-element.165.query_ref, ...), custom_call_target="tpu_custom_call" | custom-call | flops 2684354560 | bytes 2621440 | tf_op jit(solution)/shard_map/pallas_call | solution.py:493
  186.5 1.1 collective-permute-start.55
  189.5 7.3 %collective-permute-done.55 = bf16[2,48,1920]{2,1,0:T(8,128)(2,1)S(1)} collective-permute-done((bf16[2,48,1920]{2,1,0:T(8,128)(2,1)S(1)}, bf16[2,48,1920]{2,1,0:T(8,128)(2,1)S(1)}, u32[]{:S(2)}, u32[]{:S(2)}) %collective-permute-start.55) | collective-permute-done | bytes 368672 | tf_op jit(solution)/shard_map/ppermute | solution.py:35
  197.0 1.1 collective-permute-done.52
  198.2 1.0 pad_maximum_fusion.1
  199.4 1.1 collective-permute-start.61
  201.3 16.9 %shard_map.278 = (bf16[512,512]{1,0:T(8,128)(2,1)}, bf16[512,512]{1,0:T(8,128)(2,1)}, bf16[512,512]{1,0:T(8,128)(2,1)}, bf16[512,512]{1,0:T(8,128)(2,1)}, bf16[512,512]{1,0:T(8,128)(2,1)}) custom-call(s32[2]{0:T(128)} %compare_convert_fusion.early_ref, bf16[512,768]{1,0:T(8,128)(2,1)} %get-tuple-element.165.query_ref, ...), custom_call_target="tpu_custom_call" | custom-call | flops 5368709120 | bytes 5242880 | tf_op jit(solution)/shard_map/pallas_call | solution.py:493
  218.2 1.8 collective-permute-start.59
  223.1 1.3 concatenate.56.others
  226.3 1.2 collective-permute-done.48.refs_4_
  227.8 2.6 collective-permute-start.77
  231.1 11.0 %shard_map.279 = (bf16[4,48,1280]{2,1,0:T(8,128)(2,1)}, bf16[4,48,1280]{2,1,0:T(8,128)(2,1)}, bf16[4,48,1280]{2,1,0:T(8,128)(2,1)}, bf16[2,48,1280]{2,1,0:T(8,12...) custom-call(s32[2]{0:T(128)} %pad_add_fusion.index_ref, ...), custom_call_target="tpu_custom_call" | custom-call | flops 3623878656 | bytes 16613376 | tf_op jit(solution)/shard_map/pallas_call | solution.py:185
  242.1 1.1 collective-permute-start.63
  244.7 1.2 collective-permute-done.65
  247.9 5.9 %collective-permute-done.66 = bf16[2,48,1280]{2,1,0:T(8,128)(2,1)S(1)} collective-permute-done((bf16[2,48,1280]{2,1,0:T(8,128)(2,1)S(1)}, bf16[2,48,1280]{2,1,0:T(8,128)(2,1)S(1)}, u32[]{:S(2)}, u32[]{:S(2)}) %collective-permute-start.66) | collective-permute-done | bytes 245792 | tf_op jit(solution)/shard_map/ppermute | solution.py:35
  255.6 10.0 %collective-permute-done.67 = bf16[4,48,1280]{2,1,0:T(8,128)(2,1)S(1)} collective-permute-done((bf16[4,48,1280]{2,1,0:T(8,128)(2,1)S(1)}, bf16[4,48,1280]{2,1,0:T(8,128)(2,1)S(1)}, u32[]{:S(2)}, u32[]{:S(2)}) %collective-permute-start.67) | collective-permute-done | bytes 491552 | tf_op jit(solution)/shard_map/ppermute | solution.py:35
  266.3 1.6 collective-permute-start.72
  267.9 1.4 collective-permute-start.73
  270.2 4.2 %collective-permute-done.73 = bf16[48,1280]{1,0:T(8,128)(2,1)S(1)} collective-permute-done((bf16[48,1280]{1,0:T(8,128)(2,1)S(1)}, bf16[48,1280]{1,0:T(8,128)(2,1)S(1)}, u32[]{:S(2)}, u32[]{:S(2)}) %collective-permute-start.73) | collective-permute-done | bytes 122912 | tf_op jit(solution)/shard_map/ppermute | solution.py:35
  274.4 1.5 collective-permute-done.74
  276.0 5.3 %collective-permute-start.75 = (f32[24,1280]{1,0:T(8,128)S(1)}, f32[24,1280]{1,0:T(8,128)S(1)}, u32[]{:S(2)}, u32[]{:S(2)}) collective-permute-start(f32[24,1280]{1,0:T(8,128)S(1)} %constant_dynamic-slice_fusion.1), channel_id=1, source_target_pairs={{0,1},{1,0},{2,3},{3,2},{4,5},{5,4},{6,7},{7,6},{8,9},{9,8},{10,11... | collective-permute-start | bytes 368648 | tf_op jit(solution)/shard_map/ppermute | solution.py:39
  (278 shorter events, 45.2 us)
Async XLA Ops:
  3.4 5.2 %collective-permute-start = (bf16[1,48,1280]{2,1,0:T(8,128)(2,1)S(1)}, bf16[1,48,1280]{2,1,0:T(8,128)(2,1)S(1)}, u32[]{:S(2)}, u32[]{:S(2)}) collective-permute-start(bf16[1,48,1280]{2,1,0:T(8,128)(2,1)S(1)} %fusion.12), channel_id=1, source_target_pairs={{0,8},{2,10},{4,12},{6,14},{8,0},{10,2},{12,4},{14,6},{16,24},{18,... | collective-permute-start | bytes 368648 | tf_op jit(solution)/shard_map/ppermute | solution.py:35
  5.5 4.7 %collective-permute-start.1 = (bf16[1,48,1280]{2,1,0:T(8,128)(2,1)S(1)}, bf16[1,48,1280]{2,1,0:T(8,128)(2,1)S(1)}, u32[]{:S(2)}, u32[]{:S(2)}) collective-permute-start(bf16[1,48,1280]{2,1,0:T(8,128)(2,1)S(1)} %fusion.12), channel_id=1, source_target_pairs={{0,16},{2,18},{4,20},{6,22},{8,24},{10,26},{12,28},{14,30},{16,0},... | collective-permute-start | bytes 368648 | tf_op jit(solution)/shard_map/ppermute | solution.py:35
  7.9 7.9 %collective-permute-start.2 = (bf16[1,48,1280]{2,1,0:T(8,128)(2,1)S(1)}, bf16[1,48,1280]{2,1,0:T(8,128)(2,1)S(1)}, u32[]{:S(2)}, u32[]{:S(2)}) collective-permute-start(bf16[1,48,1280]{2,1,0:T(8,128)(2,1)S(1)} %fusion.12), channel_id=1, source_target_pairs={{0,24},{2,26},{4,28},{6,30},{8,16},{10,18},{12,20},{14,22},{16,8},... | collective-permute-start | bytes 368648 | tf_op jit(solution)/shard_map/ppermute | solution.py:35
  15.8 9.8 %collective-permute-start.4 = (bf16[4,48,1280]{2,1,0:T(8,128)(2,1)S(1)}, bf16[4,48,1280]{2,1,0:T(8,128)(2,1)}, u32[]{:S(2)}, u32[]{:S(2)}) collective-permute-start(bf16[4,48,1280]{2,1,0:T(8,128)(2,1)S(1)} %pad_maximum_fusion.6.refs_0_), channel_id=1, source_target_pairs={{0,4},{2,6},{4,0},{6,2},{8,12},{10,14},{12,8},{14,10},{16,20},{18,... | collective-permute-start | bytes 1474568 | tf_op jit(solution)/shard_map/ppermute | solution.py:35
  17.2 10.8 %collective-permute-start.3 = (bf16[4,48,1280]{2,1,0:T(8,128)(2,1)S(1)}, bf16[4,48,1280]{2,1,0:T(8,128)(2,1)}, u32[]{:S(2)}, u32[]{:S(2)}) collective-permute-start(bf16[4,48,1280]{2,1,0:T(8,128)(2,1)S(1)} %pad_maximum_fusion.6.refs_0_), channel_id=1, source_target_pairs={{0,2},{2,0},{4,6},{6,4},{8,10},{10,8},{12,14},{14,12},{16,18},{18,... | collective-permute-start | bytes 1474568 | tf_op jit(solution)/shard_map/ppermute | solution.py:35
  19.4 10.8 %collective-permute-start.7 = (bf16[1,48,1920]{2,1,0:T(8,128)(2,1)S(1)}, bf16[1,48,1920]{2,1,0:T(8,128)(2,1)S(1)}, u32[]{:S(2)}, u32[]{:S(2)}) collective-permute-start(bf16[1,48,1920]{2,1,0:T(8,128)(2,1)S(1)} %dynamic-slice_bitcast_fusion), channel_id=1, source_target_pairs={{0,8},{2,10},{4,12},{6,14},{8,0},{10,2},{12,4},{14,6},{16,24},{18,... | collective-permute-start | bytes 552968 | tf_op jit(solution)/shard_map/ppermute | solution.py:35
  22.0 8.2 %collective-permute-start.8 = (bf16[1,48,1920]{2,1,0:T(8,128)(2,1)S(1)}, bf16[1,48,1920]{2,1,0:T(8,128)(2,1)S(1)}, u32[]{:S(2)}, u32[]{:S(2)}) collective-permute-start(bf16[1,48,1920]{2,1,0:T(8,128)(2,1)S(1)} %dynamic-slice_bitcast_fusion), channel_id=1, source_target_pairs={{0,16},{2,18},{4,20},{6,22},{8,24},{10,26},{12,28},{14,30},{16,0},... | collective-permute-start | bytes 552968 | tf_op jit(solution)/shard_map/ppermute | solution.py:35
  23.5 11.2 %collective-permute-start.9 = (bf16[1,48,1920]{2,1,0:T(8,128)(2,1)S(1)}, bf16[1,48,1920]{2,1,0:T(8,128)(2,1)S(1)}, u32[]{:S(2)}, u32[]{:S(2)}) collective-permute-start(bf16[1,48,1920]{2,1,0:T(8,128)(2,1)S(1)} %dynamic-slice_bitcast_fusion), channel_id=1, source_target_pairs={{0,24},{2,26},{4,28},{6,30},{8,16},{10,18},{12,20},{14,22},{16,8},... | collective-permute-start | bytes 552968 | tf_op jit(solution)/shard_map/ppermute | solution.py:35
  26.6 8.2 %collective-permute-start.5 = (bf16[2,48,1280]{2,1,0:T(8,128)(2,1)S(1)}, bf16[2,48,1280]{2,1,0:T(8,128)(2,1)S(1)}, u32[]{:S(2)}, u32[]{:S(2)}) collective-permute-start(bf16[2,48,1280]{2,1,0:T(8,128)(2,1)S(1)} %slice.252), channel_id=1, source_target_pairs={{0,2},{2,0},{4,6},{6,4},{8,10},{10,8},{12,14},{14,12},{16,18},{18,... | collective-permute-start | bytes 737288 | tf_op jit(solution)/shard_map/ppermute | solution.py:35
  28.9 6.0 %collective-permute-start.6 = (bf16[2,48,1280]{2,1,0:T(8,128)(2,1)S(1)}, bf16[2,48,1280]{2,1,0:T(8,128)(2,1)S(1)}, u32[]{:S(2)}, u32[]{:S(2)}) collective-permute-start(bf16[2,48,1280]{2,1,0:T(8,128)(2,1)S(1)} %slice.253), channel_id=1, source_target_pairs={{0,4},{2,6},{4,0},{6,2},{8,12},{10,14},{12,8},{14,10},{16,20},{18,... | collective-permute-start | bytes 737288 | tf_op jit(solution)/shard_map/ppermute | solution.py:35
  34.9 9.2 %collective-permute-start.10 = (bf16[4,48,1280]{2,1,0:T(8,128)(2,1)S(1)}, bf16[4,48,1280]{2,1,0:T(8,128)(2,1)}, u32[]{:S(2)}, u32[]{:S(2)}) collective-permute-start(bf16[4,48,1280]{2,1,0:T(8,128)(2,1)S(1)} %pad_maximum_fusion.6.refs_0_), channel_id=1, source_target_pairs={{0,1},{1,0},{2,3},{3,2},{4,5},{5,4},{6,7},{7,6},{8,9},{9,8},{10,11... | collective-permute-start | bytes 1474568 | tf_op jit(solution)/shard_map/ppermute | solution.py:39
  43.2 30.7 %collective-permute-start.17 = (bf16[4,48,1920]{2,1,0:T(8,128)(2,1)S(1)}, bf16[4,48,1920]{2,1,0:T(8,128)(2,1)S(1)}, u32[]{:S(2)}, u32[]{:S(2)}) collective-permute-start(bf16[4,48,1920]{2,1,0:T(8,128)(2,1)S(1)} %pad_maximum_fusion.refs_0_), channel_id=1, source_target_pairs={{0,2},{2,0},{4,6},{6,4},{8,10},{10,8},{12,14},{14,12},{16,18},{18,... | collective-permute-start | bytes 2211848 | tf_op jit(solution)/shard_map/ppermute | solution.py:35
  43.5 30.5 %collective-permute-start.18 = (bf16[4,48,1920]{2,1,0:T(8,128)(2,1)S(1)}, bf16[4,48,1920]{2,1,0:T(8,128)(2,1)S(1)}, u32[]{:S(2)}, u32[]{:S(2)}) collective-permute-start(bf16[4,48,1920]{2,1,0:T(8,128)(2,1)S(1)} %pad_maximum_fusion.refs_0_), channel_id=1, source_target_pairs={{0,4},{2,6},{4,0},{6,2},{8,12},{10,14},{12,8},{14,10},{16,20},{18,... | collective-permute-start | bytes 2211848 | tf_op jit(solution)/shard_map/ppermute | solution.py:35
  51.3 22.7 %collective-permute-start.15 = (bf16[512,768]{1,0:T(8,128)(2,1)}, bf16[512,768]{1,0:T(8,128)(2,1)}, u32[]{:S(2)}, u32[]{:S(2)}) collective-permute-start(bf16[512,768]{1,0:T(8,128)(2,1)} %get-tuple-element.170.own_key), channel_id=1, source_target_pairs={{0,1},{1,0},{2,3},{3,2},{4,5},{5,4},{6,7},{7,6},{8,9},{9,8},{10,11... | collective-permute-start | bytes 2359304 | tf_op jit(solution)/shard_map/ppermute | solution.py:39
  52.0 22.0 %collective-permute-start.16 = (bf16[512,768]{1,0:T(8,128)(2,1)}, bf16[512,768]{1,0:T(8,128)(2,1)}, u32[]{:S(2)}, u32[]{:S(2)}) collective-permute-start(bf16[512,768]{1,0:T(8,128)(2,1)} %get-tuple-element.171.own_value), channel_id=1, source_target_pairs={{0,1},{1,0},{2,3},{3,2},{4,5},{5,4},{6,7},{7,6},{8,9},{9,8},{10,11... | collective-permute-start | bytes 2359304 | tf_op jit(solution)/shard_map/ppermute | solution.py:39
  52.1 6.5 %collective-permute-start.19 = (bf16[1,48,1536]{2,1,0:T(8,128)(2,1)S(1)}, bf16[1,48,1536]{2,1,0:T(8,128)(2,1)S(1)}, u32[]{:S(2)}, u32[]{:S(2)}) collective-permute-start(bf16[1,48,1536]{2,1,0:T(8,128)(2,1)S(1)} %dynamic-slice_bitcast_fusion.1), channel_id=1, source_target_pairs={{0,8},{2,10},{4,12},{6,14},{8,0},{10,2},{12,4},{14,6},{16,24},{18,... | collective-permute-start | bytes 442376 | tf_op jit(solution)/shard_map/ppermute | solution.py:35
  58.6 9.3 %collective-permute-start.20 = (bf16[1,48,1536]{2,1,0:T(8,128)(2,1)S(1)}, bf16[1,48,1536]{2,1,0:T(8,128)(2,1)S(1)}, u32[]{:S(2)}, u32[]{:S(2)}) collective-permute-start(bf16[1,48,1536]{2,1,0:T(8,128)(2,1)S(1)} %dynamic-slice_bitcast_fusion.1), channel_id=1, source_target_pairs={{0,16},{2,18},{4,20},{6,22},{8,24},{10,26},{12,28},{14,30},{16,0},... | collective-permute-start | bytes 442376 | tf_op jit(solution)/shard_map/ppermute | solution.py:35
  68.0 5.9 %collective-permute-start.21 = (bf16[1,48,1536]{2,1,0:T(8,128)(2,1)S(1)}, bf16[1,48,1536]{2,1,0:T(8,128)(2,1)S(1)}, u32[]{:S(2)}, u32[]{:S(2)}) collective-permute-start(bf16[1,48,1536]{2,1,0:T(8,128)(2,1)S(1)} %dynamic-slice_bitcast_fusion.1), channel_id=1, source_target_pairs={{0,24},{2,26},{4,28},{6,30},{8,16},{10,18},{12,20},{14,22},{16,8},... | collective-permute-start | bytes 442376 | tf_op jit(solution)/shard_map/ppermute | solution.py:35
  74.0 16.3 %collective-permute-start.22 = (bf16[2,48,1920]{2,1,0:T(8,128)(2,1)S(1)}, bf16[2,48,1920]{2,1,0:T(8,128)(2,1)S(1)}, u32[]{:S(2)}, u32[]{:S(2)}) collective-permute-start(bf16[2,48,1920]{2,1,0:T(8,128)(2,1)S(1)} %slice.192), channel_id=1, source_target_pairs={{0,2},{2,0},{4,6},{6,4},{8,10},{10,8},{12,14},{14,12},{16,18},{18,... | collective-permute-start | bytes 1105928 | tf_op jit(solution)/shard_map/ppermute | solution.py:35
  75.3 15.1 %collective-permute-start.23 = (bf16[2,48,1920]{2,1,0:T(8,128)(2,1)S(1)}, bf16[2,48,1920]{2,1,0:T(8,128)(2,1)S(1)}, u32[]{:S(2)}, u32[]{:S(2)}) collective-permute-start(bf16[2,48,1920]{2,1,0:T(8,128)(2,1)S(1)} %slice.193), channel_id=1, source_target_pairs={{0,4},{2,6},{4,0},{6,2},{8,12},{10,14},{12,8},{14,10},{16,20},{18,... | collective-permute-start | bytes 1105928 | tf_op jit(solution)/shard_map/ppermute | solution.py:35
  90.4 9.3 %collective-permute-start.24 = (bf16[4,48,1920]{2,1,0:T(8,128)(2,1)S(1)}, bf16[4,48,1920]{2,1,0:T(8,128)(2,1)}, u32[]{:S(2)}, u32[]{:S(2)}) collective-permute-start(bf16[4,48,1920]{2,1,0:T(8,128)(2,1)S(1)} %pad_maximum_fusion.refs_0_), channel_id=1, source_target_pairs={{0,1},{1,0},{2,3},{3,2},{4,5},{5,4},{6,7},{7,6},{8,9},{9,8},{10,11... | collective-permute-start | bytes 2211848 | tf_op jit(solution)/shard_map/ppermute | solution.py:39
  93.4 6.4 %collective-permute-start.25 = (bf16[4,48,1920]{2,1,0:T(8,128)(2,1)S(1)}, bf16[4,48,1920]{2,1,0:T(8,128)(2,1)}, u32[]{:S(2)}, u32[]{:S(2)}) collective-permute-start(bf16[4,48,1920]{2,1,0:T(8,128)(2,1)S(1)} %collective-permute-done.17.refs_1_), channel_id=1, source_target_pairs={{0,1},{1,0},{2,3},{3,2},{4,5},{5,4},{6,7},{7,6},{8,9},{9,8},{10,11... | collective-permute-start | bytes 2211848 | tf_op jit(solution)/shard_map/ppermute | solution.py:39
  93.5 6.3 %collective-permute-start.26 = (bf16[4,48,1920]{2,1,0:T(8,128)(2,1)S(1)}, bf16[4,48,1920]{2,1,0:T(8,128)(2,1)}, u32[]{:S(2)}, u32[]{:S(2)}) collective-permute-start(bf16[4,48,1920]{2,1,0:T(8,128)(2,1)S(1)} %collective-permute-done.18.refs_2_), channel_id=1, source_target_pairs={{0,1},{1,0},{2,3},{3,2},{4,5},{5,4},{6,7},{7,6},{8,9},{9,8},{10,11... | collective-permute-start | bytes 2211848 | tf_op jit(solution)/shard_map/ppermute | solution.py:39
  96.3 16.5 %collective-permute-start.29 = (bf16[4,48,1536]{2,1,0:T(8,128)(2,1)S(1)}, bf16[4,48,1536]{2,1,0:T(8,128)(2,1)}, u32[]{:S(2)}, u32[]{:S(2)}) collective-permute-start(bf16[4,48,1536]{2,1,0:T(8,128)(2,1)S(1)} %pad_maximum_fusion.3.refs_0_), channel_id=1, source_target_pairs={{0,2},{2,0},{4,6},{6,4},{8,10},{10,8},{12,14},{14,12},{16,18},{18,... | collective-permute-start | bytes 1769480 | tf_op jit(solution)/shard_map/ppermute | solution.py:35
  97.3 15.4 %collective-permute-start.30 = (bf16[4,48,1536]{2,1,0:T(8,128)(2,1)S(1)}, bf16[4,48,1536]{2,1,0:T(8,128)(2,1)}, u32[]{:S(2)}, u32[]{:S(2)}) collective-permute-start(bf16[4,48,1536]{2,1,0:T(8,128)(2,1)S(1)} %pad_maximum_fusion.3.refs_0_), channel_id=1, source_target_pairs={{0,4},{2,6},{4,0},{6,2},{8,12},{10,14},{12,8},{14,10},{16,20},{18,... | collective-permute-start | bytes 1769480 | tf_op jit(solution)/shard_map/ppermute | solution.py:35
  113.7 9.2 %collective-permute-start.31 = (bf16[2,48,1536]{2,1,0:T(8,128)(2,1)S(1)}, bf16[2,48,1536]{2,1,0:T(8,128)(2,1)S(1)}, u32[]{:S(2)}, u32[]{:S(2)}) collective-permute-start(bf16[2,48,1536]{2,1,0:T(8,128)(2,1)S(1)} %slice.195), channel_id=1, source_target_pairs={{0,2},{2,0},{4,6},{6,4},{8,10},{10,8},{12,14},{14,12},{16,18},{18,... | collective-permute-start | bytes 884744 | tf_op jit(solution)/shard_map/ppermute | solution.py:35
  115.2 7.8 %collective-permute-start.32 = (bf16[2,48,1536]{2,1,0:T(8,128)(2,1)S(1)}, bf16[2,48,1536]{2,1,0:T(8,128)(2,1)S(1)}, u32[]{:S(2)}, u32[]{:S(2)}) collective-permute-start(bf16[2,48,1536]{2,1,0:T(8,128)(2,1)S(1)} %slice.196), channel_id=1, source_target_pairs={{0,4},{2,6},{4,0},{6,2},{8,12},{10,14},{12,8},{14,10},{16,20},{18,... | collective-permute-start | bytes 884744 | tf_op jit(solution)/shard_map/ppermute | solution.py:35
  124.7 5.8 %collective-permute-start.42 = (bf16[4,48,1536]{2,1,0:T(8,128)(2,1)}, bf16[4,48,1536]{2,1,0:T(8,128)(2,1)S(1)}, u32[]{:S(2)}, u32[]{:S(2)}) collective-permute-start(bf16[4,48,1536]{2,1,0:T(8,128)(2,1)} %get-tuple-element.227), channel_id=1, source_target_pairs={{0,1},{1,0},{2,3},{3,2},{4,5},{5,4},{6,7},{7,6},{8,9},{9,8},{10,11... | collective-permute-start | bytes 1769480 | tf_op jit(solution)/shard_map/ppermute | solution.py:39
  124.7 6.2 %collective-permute-start.39 = (bf16[4,48,1536]{2,1,0:T(8,128)(2,1)}, bf16[4,48,1536]{2,1,0:T(8,128)(2,1)S(1)}, u32[]{:S(2)}, u32[]{:S(2)}) collective-permute-start(bf16[4,48,1536]{2,1,0:T(8,128)(2,1)} %get-tuple-element.223), channel_id=1, source_target_pairs={{0,1},{1,0},{2,3},{3,2},{4,5},{5,4},{6,7},{7,6},{8,9},{9,8},{10,11... | collective-permute-start | bytes 1769480 | tf_op jit(solution)/shard_map/ppermute | solution.py:39
  125.2 8.5 %collective-permute-start.33 = (bf16[4,48,1536]{2,1,0:T(8,128)(2,1)S(1)}, bf16[4,48,1536]{2,1,0:T(8,128)(2,1)S(1)}, u32[]{:S(2)}, u32[]{:S(2)}) collective-permute-start(bf16[4,48,1536]{2,1,0:T(8,128)(2,1)S(1)} %pad_maximum_fusion.3.refs_0_), channel_id=1, source_target_pairs={{0,1},{1,0},{2,3},{3,2},{4,5},{5,4},{6,7},{7,6},{8,9},{9,8},{10,11... | collective-permute-start | bytes 1769480 | tf_op jit(solution)/shard_map/ppermute | solution.py:39
  126.1 8.4 %collective-permute-start.34 = (bf16[4,48,1536]{2,1,0:T(8,128)(2,1)}, bf16[4,48,1536]{2,1,0:T(8,128)(2,1)S(1)}, u32[]{:S(2)}, u32[]{:S(2)}) collective-permute-start(bf16[4,48,1536]{2,1,0:T(8,128)(2,1)} %collective-permute-done.29.refs_1_), channel_id=1, source_target_pairs={{0,1},{1,0},{2,3},{3,2},{4,5},{5,4},{6,7},{7,6},{8,9},{9,8},{10,11... | collective-permute-start | bytes 1769480 | tf_op jit(solution)/shard_map/ppermute | solution.py:39
  129.0 5.5 %collective-permute-start.35 = (bf16[4,48,1536]{2,1,0:T(8,128)(2,1)}, bf16[4,48,1536]{2,1,0:T(8,128)(2,1)S(1)}, u32[]{:S(2)}, u32[]{:S(2)}) collective-permute-start(bf16[4,48,1536]{2,1,0:T(8,128)(2,1)} %collective-permute-done.30.refs_2_), channel_id=1, source_target_pairs={{0,1},{1,0},{2,3},{3,2},{4,5},{5,4},{6,7},{7,6},{8,9},{9,8},{10,11... | collective-permute-start | bytes 1769480 | tf_op jit(solution)/shard_map/ppermute | solution.py:39
  132.1 21.9 %collective-permute-start.38 = (bf16[4,48,1536]{2,1,0:T(8,128)(2,1)S(1)}, bf16[4,48,1536]{2,1,0:T(8,128)(2,1)S(1)}, u32[]{:S(2)}, u32[]{:S(2)}) collective-permute-start(bf16[4,48,1536]{2,1,0:T(8,128)(2,1)S(1)} %copy-done.25), channel_id=1, source_target_pairs={{0,1},{1,0},{2,3},{3,2},{4,5},{5,4},{6,7},{7,6},{8,9},{9,8},{10,11... | collective-permute-start | bytes 1769480 | tf_op jit(solution)/shard_map/ppermute | solution.py:39
  132.7 21.6 %collective-permute-start.44 = (bf16[2,48,1536]{2,1,0:T(8,128)(2,1)S(1)}, bf16[2,48,1536]{2,1,0:T(8,128)(2,1)S(1)}, u32[]{:S(2)}, u32[]{:S(2)}) collective-permute-start(bf16[2,48,1536]{2,1,0:T(8,128)(2,1)S(1)} %add_convert_fusion.14), channel_id=1, source_target_pairs={{0,2},{2,0},{4,6},{6,4},{8,10},{10,8},{12,14},{14,12},{16,18},{18,... | collective-permute-start | bytes 884744 | tf_op jit(solution)/shard_map/ppermute | solution.py:35
  133.7 20.7 %collective-permute-start.41 = (bf16[2,48,1536]{2,1,0:T(8,128)(2,1)S(1)}, bf16[2,48,1536]{2,1,0:T(8,128)(2,1)S(1)}, u32[]{:S(2)}, u32[]{:S(2)}) collective-permute-start(bf16[2,48,1536]{2,1,0:T(8,128)(2,1)S(1)} %add_convert_fusion.16), channel_id=1, source_target_pairs={{0,4},{2,6},{4,0},{6,2},{8,12},{10,14},{12,8},{14,10},{16,20},{18,... | collective-permute-start | bytes 884744 | tf_op jit(solution)/shard_map/ppermute | solution.py:35
  154.5 14.0 %collective-permute-start.45 = (bf16[4,48,1536]{2,1,0:T(8,128)(2,1)S(1)}, bf16[4,48,1536]{2,1,0:T(8,128)(2,1)S(1)}, u32[]{:S(2)}, u32[]{:S(2)}) collective-permute-start(bf16[4,48,1536]{2,1,0:T(8,128)(2,1)S(1)} %pad_maximum_fusion.4), channel_id=1, source_target_pairs={{0,2},{2,0},{4,6},{6,4},{8,10},{10,8},{12,14},{14,12},{16,18},{18,... | collective-permute-start | bytes 1769480 | tf_op jit(solution)/shard_map/ppermute | solution.py:35
  155.0 13.6 %collective-permute-start.46 = (bf16[4,48,1536]{2,1,0:T(8,128)(2,1)S(1)}, bf16[4,48,1536]{2,1,0:T(8,128)(2,1)S(1)}, u32[]{:S(2)}, u32[]{:S(2)}) collective-permute-start(bf16[4,48,1536]{2,1,0:T(8,128)(2,1)S(1)} %pad_maximum_fusion.5), channel_id=1, source_target_pairs={{0,4},{2,6},{4,0},{6,2},{8,12},{10,14},{12,8},{14,10},{16,20},{18,... | collective-permute-start | bytes 1769480 | tf_op jit(solution)/shard_map/ppermute | solution.py:35
  169.1 16.2 %collective-permute-start.56 = (bf16[48,1536]{1,0:T(8,128)(2,1)S(1)}, bf16[48,1536]{1,0:T(8,128)(2,1)S(1)}, u32[]{:S(2)}, u32[]{:S(2)}) collective-permute-start(bf16[48,1536]{1,0:T(8,128)(2,1)S(1)} %get-tuple-element.263), channel_id=1, source_target_pairs={{0,8},{2,10},{4,12},{6,14},{8,0},{10,2},{12,4},{14,6},{16,24},{18,... | collective-permute-start | bytes 442376 | tf_op jit(solution)/shard_map/ppermute | solution.py:35
  170.3 15.5 %collective-permute-start.57 = (bf16[48,1536]{1,0:T(8,128)(2,1)S(1)}, bf16[48,1536]{1,0:T(8,128)(2,1)S(1)}, u32[]{:S(2)}, u32[]{:S(2)}) collective-permute-start(bf16[48,1536]{1,0:T(8,128)(2,1)S(1)} %get-tuple-element.264), channel_id=1, source_target_pairs={{0,16},{2,18},{4,20},{6,22},{8,24},{10,26},{12,28},{14,30},{16,0},... | collective-permute-start | bytes 442376 | tf_op jit(solution)/shard_map/ppermute | solution.py:35
  172.0 13.8 %collective-permute-start.58 = (bf16[48,1536]{1,0:T(8,128)(2,1)S(1)}, bf16[48,1536]{1,0:T(8,128)(2,1)S(1)}, u32[]{:S(2)}, u32[]{:S(2)}) collective-permute-start(bf16[48,1536]{1,0:T(8,128)(2,1)S(1)} %get-tuple-element.265), channel_id=1, source_target_pairs={{0,24},{2,26},{4,28},{6,30},{8,16},{10,18},{12,20},{14,22},{16,8},... | collective-permute-start | bytes 442376 | tf_op jit(solution)/shard_map/ppermute | solution.py:35
  172.7 13.7 %collective-permute-start.54 = (bf16[2,48,1920]{2,1,0:T(8,128)(2,1)S(1)}, bf16[2,48,1920]{2,1,0:T(8,128)(2,1)S(1)}, u32[]{:S(2)}, u32[]{:S(2)}) collective-permute-start(bf16[2,48,1920]{2,1,0:T(8,128)(2,1)S(1)} %copy-done.30), channel_id=1, source_target_pairs={{0,1},{1,0},{2,3},{3,2},{4,5},{5,4},{6,7},{7,6},{8,9},{9,8},{10,11... | collective-permute-start | bytes 1105928 | tf_op jit(solution)/shard_map/ppermute | solution.py:39
  175.7 13.4 %collective-permute-start.53 = (bf16[4,48,1920]{2,1,0:T(8,128)(2,1)S(1)}, bf16[4,48,1920]{2,1,0:T(8,128)(2,1)S(1)}, u32[]{:S(2)}, u32[]{:S(2)}) collective-permute-start(bf16[4,48,1920]{2,1,0:T(8,128)(2,1)S(1)} %copy-done.24), channel_id=1, source_target_pairs={{0,1},{1,0},{2,3},{3,2},{4,5},{5,4},{6,7},{7,6},{8,9},{9,8},{10,11... | collective-permute-start | bytes 2211848 | tf_op jit(solution)/shard_map/ppermute | solution.py:39
  185.3 4.0 %collective-permute-start.50 = (bf16[4,48,1920]{2,1,0:T(8,128)(2,1)S(1)}, bf16[4,48,1920]{2,1,0:T(8,128)(2,1)S(1)}, u32[]{:S(2)}, u32[]{:S(2)}) collective-permute-start(bf16[4,48,1920]{2,1,0:T(8,128)(2,1)S(1)} %copy-done.23), channel_id=1, source_target_pairs={{0,1},{1,0},{2,3},{3,2},{4,5},{5,4},{6,7},{7,6},{8,9},{9,8},{10,11... | collective-permute-start | bytes 2211848 | tf_op jit(solution)/shard_map/ppermute | solution.py:39
  185.9 13.3 %collective-permute-start.49 = (bf16[4,48,1920]{2,1,0:T(8,128)(2,1)S(1)}, bf16[4,48,1920]{2,1,0:T(8,128)(2,1)S(1)}, u32[]{:S(2)}, u32[]{:S(2)}) collective-permute-start(bf16[4,48,1920]{2,1,0:T(8,128)(2,1)S(1)} %copy-done.22), channel_id=1, source_target_pairs={{0,1},{1,0},{2,3},{3,2},{4,5},{5,4},{6,7},{7,6},{8,9},{9,8},{10,11... | collective-permute-start | bytes 2211848 | tf_op jit(solution)/shard_map/ppermute | solution.py:39
  186.5 10.2 %collective-permute-start.55 = (bf16[2,48,1920]{2,1,0:T(8,128)(2,1)S(1)}, bf16[2,48,1920]{2,1,0:T(8,128)(2,1)S(1)}, u32[]{:S(2)}, u32[]{:S(2)}) collective-permute-start(bf16[2,48,1920]{2,1,0:T(8,128)(2,1)S(1)} %add_convert_fusion.10), channel_id=1, source_target_pairs={{0,2},{2,0},{4,6},{6,4},{8,10},{10,8},{12,14},{14,12},{16,18},{18,... | collective-permute-start | bytes 1105928 | tf_op jit(solution)/shard_map/ppermute | solution.py:35
  188.3 9.9 %collective-permute-start.52 = (bf16[2,48,1920]{2,1,0:T(8,128)(2,1)S(1)}, bf16[2,48,1920]{2,1,0:T(8,128)(2,1)S(1)}, u32[]{:S(2)}, u32[]{:S(2)}) collective-permute-start(bf16[2,48,1920]{2,1,0:T(8,128)(2,1)S(1)} %add_convert_fusion.12), channel_id=1, source_target_pairs={{0,4},{2,6},{4,0},{6,2},{8,12},{10,14},{12,8},{14,10},{16,20},{18,... | collective-permute-start | bytes 1105928 | tf_op jit(solution)/shard_map/ppermute | solution.py:35
  199.4 26.3 %collective-permute-start.61 = (bf16[4,48,1920]{2,1,0:T(8,128)(2,1)}, bf16[4,48,1920]{2,1,0:T(8,128)(2,1)S(1)}, u32[]{:S(2)}, u32[]{:S(2)}) collective-permute-start(bf16[4,48,1920]{2,1,0:T(8,128)(2,1)} %pad_maximum_fusion.1), channel_id=1, source_target_pairs={{0,2},{2,0},{4,6},{6,4},{8,10},{10,8},{12,14},{14,12},{16,18},{18,... | collective-permute-start | bytes 2211848 | tf_op jit(solution)/shard_map/ppermute | solution.py:35
  200.5 25.3 %collective-permute-start.62 = (bf16[4,48,1920]{2,1,0:T(8,128)(2,1)S(1)}, bf16[4,48,1920]{2,1,0:T(8,128)(2,1)S(1)}, u32[]{:S(2)}, u32[]{:S(2)}) collective-permute-start(bf16[4,48,1920]{2,1,0:T(8,128)(2,1)S(1)} %pad_maximum_fusion.2), channel_id=1, source_target_pairs={{0,4},{2,6},{4,0},{6,2},{8,12},{10,14},{12,8},{14,10},{16,20},{18,... | collective-permute-start | bytes 2211848 | tf_op jit(solution)/shard_map/ppermute | solution.py:35
  218.2 9.3 %collective-permute-start.59 = (bf16[512,512]{1,0:T(8,128)(2,1)}, bf16[512,512]{1,0:T(8,128)(2,1)}, u32[]{:S(2)}, u32[]{:S(2)}) collective-permute-start(bf16[512,512]{1,0:T(8,128)(2,1)} %get-tuple-element.269), channel_id=1, source_target_pairs={{0,1},{1,0},{2,3},{3,2},{4,5},{5,4},{6,7},{7,6},{8,9},{9,8},{10,11... | collective-permute-start | bytes 1572872 | tf_op jit(solution)/shard_map/ppermute | solution.py:39
  220.0 7.5 %collective-permute-start.60 = (bf16[512,512]{1,0:T(8,128)(2,1)}, bf16[512,512]{1,0:T(8,128)(2,1)}, u32[]{:S(2)}, u32[]{:S(2)}) collective-permute-start(bf16[512,512]{1,0:T(8,128)(2,1)} %get-tuple-element.271), channel_id=1, source_target_pairs={{0,1},{1,0},{2,3},{3,2},{4,5},{5,4},{6,7},{7,6},{8,9},{9,8},{10,11... | collective-permute-start | bytes 1572872 | tf_op jit(solution)/shard_map/ppermute | solution.py:39
  227.5 15.8 %collective-permute-start.76 = (bf16[48,1920]{1,0:T(8,128)(2,1)S(1)}, bf16[48,1920]{1,0:T(8,128)(2,1)S(1)}, u32[]{:S(2)}, u32[]{:S(2)}) collective-permute-start(bf16[48,1920]{1,0:T(8,128)(2,1)S(1)} %get-tuple-element.297), channel_id=1, source_target_pairs={{0,8},{2,10},{4,12},{6,14},{8,0},{10,2},{12,4},{14,6},{16,24},{18,... | collective-permute-start | bytes 552968 | tf_op jit(solution)/shard_map/ppermute | solution.py:35
  227.8 15.9 %collective-permute-start.77 = (bf16[48,1920]{1,0:T(8,128)(2,1)S(1)}, bf16[48,1920]{1,0:T(8,128)(2,1)S(1)}, u32[]{:S(2)}, u32[]{:S(2)}) collective-permute-start(bf16[48,1920]{1,0:T(8,128)(2,1)S(1)} %get-tuple-element.298), channel_id=1, source_target_pairs={{0,16},{2,18},{4,20},{6,22},{8,24},{10,26},{12,28},{14,30},{16,0},... | collective-permute-start | bytes 552968 | tf_op jit(solution)/shard_map/ppermute | solution.py:35
  230.4 14.1 %collective-permute-start.78 = (bf16[48,1920]{1,0:T(8,128)(2,1)S(1)}, bf16[48,1920]{1,0:T(8,128)(2,1)S(1)}, u32[]{:S(2)}, u32[]{:S(2)}) collective-permute-start(bf16[48,1920]{1,0:T(8,128)(2,1)S(1)} %get-tuple-element.299), channel_id=1, source_target_pairs={{0,24},{2,26},{4,28},{6,30},{8,16},{10,18},{12,20},{14,22},{16,8},... | collective-permute-start | bytes 552968 | tf_op jit(solution)/shard_map/ppermute | solution.py:35
  242.1 13.4 %collective-permute-start.63 = (bf16[4,48,1280]{2,1,0:T(8,128)(2,1)}, bf16[4,48,1280]{2,1,0:T(8,128)(2,1)S(1)}, u32[]{:S(2)}, u32[]{:S(2)}) collective-permute-start(bf16[4,48,1280]{2,1,0:T(8,128)(2,1)} %get-tuple-element.287), channel_id=1, source_target_pairs={{0,1},{1,0},{2,3},{3,2},{4,5},{5,4},{6,7},{7,6},{8,9},{9,8},{10,11... | collective-permute-start | bytes 1474568 | tf_op jit(solution)/shard_map/ppermute | solution.py:39
  243.1 4.1 %collective-permute-start.64 = (bf16[4,48,1280]{2,1,0:T(8,128)(2,1)}, bf16[4,48,1280]{2,1,0:T(8,128)(2,1)S(1)}, u32[]{:S(2)}, u32[]{:S(2)}) collective-permute-start(bf16[4,48,1280]{2,1,0:T(8,128)(2,1)} %get-tuple-element.289), channel_id=1, source_target_pairs={{0,1},{1,0},{2,3},{3,2},{4,5},{5,4},{6,7},{7,6},{8,9},{9,8},{10,11... | collective-permute-start | bytes 1474568 | tf_op jit(solution)/shard_map/ppermute | solution.py:39
  244.5 9.8 %collective-permute-start.68 = (bf16[4,48,1280]{2,1,0:T(8,128)(2,1)}, bf16[4,48,1280]{2,1,0:T(8,128)(2,1)S(1)}, u32[]{:S(2)}, u32[]{:S(2)}) collective-permute-start(bf16[4,48,1280]{2,1,0:T(8,128)(2,1)} %get-tuple-element.293), channel_id=1, source_target_pairs={{0,1},{1,0},{2,3},{3,2},{4,5},{5,4},{6,7},{7,6},{8,9},{9,8},{10,11... | collective-permute-start | bytes 1474568 | tf_op jit(solution)/shard_map/ppermute | solution.py:39
  245.9 24.1 %collective-permute-start.79 = (f32[24,1920]{1,0:T(8,128)S(1)}, f32[24,1920]{1,0:T(8,128)S(1)}, u32[]{:S(2)}, u32[]{:S(2)}) collective-permute-start(f32[24,1920]{1,0:T(8,128)S(1)} %constant_dynamic-slice_fusion), channel_id=1, source_target_pairs={{0,1},{1,0},{2,3},{3,2},{4,5},{5,4},{6,7},{7,6},{8,9},{9,8},{10,11... | collective-permute-start | bytes 552968 | tf_op jit(solution)/shard_map/ppermute | solution.py:39
  246.4 7.4 %collective-permute-start.66 = (bf16[2,48,1280]{2,1,0:T(8,128)(2,1)S(1)}, bf16[2,48,1280]{2,1,0:T(8,128)(2,1)S(1)}, u32[]{:S(2)}, u32[]{:S(2)}) collective-permute-start(bf16[2,48,1280]{2,1,0:T(8,128)(2,1)S(1)} %add_convert_fusion.20), channel_id=1, source_target_pairs={{0,4},{2,6},{4,0},{6,2},{8,12},{10,14},{12,8},{14,10},{16,20},{18,... | collective-permute-start | bytes 737288 | tf_op jit(solution)/shard_map/ppermute | solution.py:35
  247.2 7.3 %collective-permute-start.70 = (bf16[2,48,1280]{2,1,0:T(8,128)(2,1)S(1)}, bf16[2,48,1280]{2,1,0:T(8,128)(2,1)S(1)}, u32[]{:S(2)}, u32[]{:S(2)}) collective-permute-start(bf16[2,48,1280]{2,1,0:T(8,128)(2,1)S(1)} %add_convert_fusion.18), channel_id=1, source_target_pairs={{0,2},{2,0},{4,6},{6,4},{8,10},{10,8},{12,14},{14,12},{16,18},{18,... | collective-permute-start | bytes 737288 | tf_op jit(solution)/shard_map/ppermute | solution.py:35
  253.9 11.8 %collective-permute-start.67 = (bf16[4,48,1280]{2,1,0:T(8,128)(2,1)S(1)}, bf16[4,48,1280]{2,1,0:T(8,128)(2,1)S(1)}, u32[]{:S(2)}, u32[]{:S(2)}) collective-permute-start(bf16[4,48,1280]{2,1,0:T(8,128)(2,1)S(1)} %pad_maximum_fusion.7), channel_id=1, source_target_pairs={{0,2},{2,0},{4,6},{6,4},{8,10},{10,8},{12,14},{14,12},{16,18},{18,... | collective-permute-start | bytes 1474568 | tf_op jit(solution)/shard_map/ppermute | solution.py:35
  254.7 11.5 %collective-permute-start.71 = (bf16[4,48,1280]{2,1,0:T(8,128)(2,1)S(1)}, bf16[4,48,1280]{2,1,0:T(8,128)(2,1)S(1)}, u32[]{:S(2)}, u32[]{:S(2)}) collective-permute-start(bf16[4,48,1280]{2,1,0:T(8,128)(2,1)S(1)} %pad_maximum_fusion.8), channel_id=1, source_target_pairs={{0,4},{2,6},{4,0},{6,2},{8,12},{10,14},{12,8},{14,10},{16,20},{18,... | collective-permute-start | bytes 1474568 | tf_op jit(solution)/shard_map/ppermute | solution.py:35
  267.9 6.5 %collective-permute-start.73 = (bf16[48,1280]{1,0:T(8,128)(2,1)S(1)}, bf16[48,1280]{1,0:T(8,128)(2,1)S(1)}, u32[]{:S(2)}, u32[]{:S(2)}) collective-permute-start(bf16[48,1280]{1,0:T(8,128)(2,1)S(1)} %get-tuple-element.319), channel_id=1, source_target_pairs={{0,16},{2,18},{4,20},{6,22},{8,24},{10,26},{12,28},{14,30},{16,0},... | collective-permute-start | bytes 368648 | tf_op jit(solution)/shard_map/ppermute | solution.py:35
  269.3 6.7 %collective-permute-start.74 = (bf16[48,1280]{1,0:T(8,128)(2,1)S(1)}, bf16[48,1280]{1,0:T(8,128)(2,1)S(1)}, u32[]{:S(2)}, u32[]{:S(2)}) collective-permute-start(bf16[48,1280]{1,0:T(8,128)(2,1)S(1)} %get-tuple-element.318), channel_id=1, source_target_pairs={{0,24},{2,26},{4,28},{6,30},{8,16},{10,18},{12,20},{14,22},{16,8},... | collective-permute-start | bytes 368648 | tf_op jit(solution)/shard_map/ppermute | solution.py:35
  276.0 6.6 %collective-permute-start.75 = (f32[24,1280]{1,0:T(8,128)S(1)}, f32[24,1280]{1,0:T(8,128)S(1)}, u32[]{:S(2)}, u32[]{:S(2)}) collective-permute-start(f32[24,1280]{1,0:T(8,128)S(1)} %constant_dynamic-slice_fusion.1), channel_id=1, source_target_pairs={{0,1},{1,0},{2,3},{3,2},{4,5},{5,4},{6,7},{7,6},{8,9},{9,8},{10,11... | collective-permute-start | bytes 368648 | tf_op jit(solution)/shard_map/ppermute | solution.py:39
  (59 other events, 504.0 us)
